TPU v7x, 32 devices: a whole 2x2x4 slice. The times are simulated.
32 devices in a mesh: dp: 2 (over y), expert: 16 (over z, x, core).
Axes of the slice: x: 2, y: 2, z: 4, core: 2. Of those that a mesh axis runs over, the one named last changes fastest.
Arguments:
- hidden_states: bfloat16 [256, 4, 4096], P('expert'), may hold values from -6 to 6
- routes: int32 [256, 4, 8], P('expert'), may hold values from 0 to 15, all different within a row; in each aligned block of 64 rows (0 to 63, 64 to 127, ..., all dimensions but the last counted through in order) at most 64 rows name the same one
- route_weight: float32 [256, 4, 8], P('expert'), may hold values from 0.05 to 1
- finish_step: int32 [256], P('expert'), may hold values from 1 to 4
- group_keep: int32 [16], P('expert'), may hold values from 0 to 1
- dest_slot: int32 [256], P('expert'), may hold values from 0 to 255, as said below
- w_gate: bfloat16 [16, 4096, 1536], P('expert', None, 'dp'), may hold values from -0.09375 to 0.09375
- w_up: bfloat16 [16, 4096, 1536], P('expert', None, 'dp'), may hold values from -0.09375 to 0.09375
- w_down: bfloat16 [16, 1536, 4096], P('expert', 'dp'), may hold values from -0.15625 to 0.15625
Outputs:
- trainer_rows: bfloat16 [256, 4, 4096], P(('dp', 'expert'))
Inputs may be any that keep to these rules, and one draw needn't show every extreme that they name: `routes`: in the 64 row-steps of one prompt group (rows g * 16 to (g + 1) * 16 - 1, all steps), no expert is named more than 64 times, a bound that some block reaches; a row names 8 different experts at each step. dest_slot is a permutation of the slots; row r of group g = r // 16 goes to a slot (d * 16 + g) * 8 + i with 0 <= d < 2 and 0 <= i < 8.
All inputs are finite; a program needn't handle non-finite values.
Results may differ from a plain program's by a relative error of at most 0.0049.
Values may be sent and summed in bfloat16 or wider, within the bound.
A program may use at most 128 MiB of HBM per device.

v0:
```python
import jax
import jax.numpy as jnp
from jax import lax
from jax.sharding import PartitionSpec as P

MOST_BASE = 16


def body(
    hidden_states, routes, route_weight, finish_step, group_keep, dest_slot, w_gate, w_up, w_down
):
    expert_count = lax.axis_size("expert")
    replica_count = lax.axis_size("dp")
    row_count, step_count, model_width = hidden_states.shape
    top_count = routes.shape[2]
    tokens = row_count * step_count
    slot_count = min(tokens, max(MOST_BASE, 2 * tokens * top_count // expert_count))
    step_ids = lax.broadcasted_iota(jnp.int32, (row_count, step_count), 1)
    live_mask = ((step_ids < finish_step[:, None]) & (group_keep[0] == 1)).reshape(tokens)
    gate_share = route_weight / jnp.sum(route_weight, axis=2, keepdims=True)
    expert_ids = lax.broadcasted_iota(jnp.int32, (1, 1, expert_count), 2)
    picked = (routes.reshape(tokens, top_count, 1) == expert_ids) & live_mask[:, None, None]
    hit_mask = jnp.sum(picked.astype(jnp.int32), axis=1)
    share_wide = jnp.broadcast_to(gate_share.reshape(tokens, top_count, 1), picked.shape)
    weight = jnp.sum(jnp.where(picked, share_wide, jnp.zeros_like(share_wide)), axis=1)
    prior_hits = jnp.cumsum(hit_mask, axis=0) - hit_mask
    slot_ids = lax.broadcasted_iota(jnp.int32, (1, 1, slot_count), 2)
    placement = (hit_mask[:, :, None] == 1) & (prior_hits[:, :, None] == slot_ids)
    weighted_place = (placement.astype(jnp.float32) * weight[:, :, None]).reshape(
        tokens, expert_count * slot_count
    )
    placement = placement.reshape(tokens, expert_count * slot_count)
    flat_inputs = hidden_states.reshape(tokens, model_width)
    outgoing = lax.dot_general(
        placement.astype(jnp.bfloat16),
        flat_inputs,
        (((0,), (0,)), ((), ())),
        preferred_element_type=jnp.float32,
    ).astype(jnp.bfloat16)
    outgoing = outgoing.reshape(expert_count, slot_count, model_width)
    arrived = lax.all_to_all(outgoing, "expert", split_axis=0, concat_axis=0, tiled=True)
    sources = arrived.shape[0]
    items = arrived.shape[1]
    flattened = arrived.reshape(sources * items, model_width)
    gate_part = jnp.dot(flattened, w_gate[0], preferred_element_type=jnp.float32)
    up_part = jnp.dot(flattened, w_up[0], preferred_element_type=jnp.float32)
    activated = (jax.nn.silu(gate_part) * up_part).astype(jnp.bfloat16)
    expert_result = jnp.dot(activated, w_down[0], preferred_element_type=jnp.float32)
    partial_out = expert_result.reshape(sources, items, model_width)
    share_rows = row_count // replica_count
    flat_device = dest_slot // share_rows
    target = flat_device // expert_count * share_rows + dest_slot % share_rows
    position_ids = lax.broadcasted_iota(jnp.int32, (replica_count * share_rows, row_count), 0)
    arrangement = (target[None, :] == position_ids).astype(jnp.float32)
    quarter = model_width // replica_count
    columns = lax.psum_scatter(partial_out, "dp", scatter_dimension=2, tiled=True)
    returned_rows = lax.all_to_all(columns, "expert", split_axis=0, concat_axis=0, tiled=True)
    combined = jnp.dot(
        weighted_place,
        returned_rows.reshape(expert_count * slot_count, quarter),
        precision=lax.Precision.HIGHEST,
        preferred_element_type=jnp.float32,
    ).astype(jnp.bfloat16)
    arranged = jnp.dot(
        arrangement.astype(jnp.bfloat16),
        combined.reshape(row_count, step_count * quarter),
        preferred_element_type=jnp.float32,
    ).astype(jnp.bfloat16)
    arranged = arranged.reshape(replica_count, share_rows, step_count, quarter)
    delivered = lax.all_to_all(arranged, "dp", split_axis=0, concat_axis=3, tiled=True)
    return delivered.reshape(share_rows, step_count, model_width)


def solution(mesh):
    in_specs = (
        P("expert", None, None),
        P("expert", None, None),
        P("expert", None, None),
        P("expert"),
        P("expert"),
        P("expert"),
        P("expert", None, "dp"),
        P("expert", None, "dp"),
        P("expert", "dp", None),
    )
    out_specs = P(("dp", "expert"), None, None)
    return jax.shard_map(body, mesh=mesh, in_specs=in_specs, out_specs=out_specs, check_vma=False)
```

profile of v0, /device:TPU:10, one launch (start us, length us, event | category | flops | bytes accessed | tf_op | source)
XLA Modules:
  0.0 631.3 jit_solution(5380412105797775694)
XLA Ops:
  6.5 0.0 reduce-scatter.2.cloned.1.call-start
  6.5 0.8 copy.17
  7.3 0.1 copy.18
  8.1 0.7 fusion.12
  8.8 0.1 and.58
  8.9 0.1 copy.20
  9.0 0.1 reduce_window_sum.11
  9.1 0.1 copy.19
  9.2 0.3 fusion.10
  9.6 0.3 and.63
  9.9 1.2 reshape.100
  11.0 0.0 slice-start
  11.0 2.4 convolution_convert_fusion.1
  13.4 0.0 slice-start.1
  13.4 0.0 slice-start.2
  13.5 188.3 %all_to_all.25 = bf16[16,64,4096]{2,1,0:T(8,128)(2,1)S(1)} all-to-all(bf16[16,64,4096]{2,1,0:T(8,128)(2,1)S(1)} %bitcast.33), channel_id=1, replica_groups=mesh['dp'=2,'expert'=16] {'expert'}, dimensions={0} | all-to-all | bytes 16777216 | tf_op jit(solution)/shard_map/all_to_all | solution.py:41
  201.7 0.0 slice-done
  201.7 0.0 slice-done.1
  201.8 0.0 slice-start.3
  201.8 6.7 %fusion.2 = f32[1024,768]{1,0:T(8,128)S(1)} fusion(bf16[1024,4096]{1,0:T(8,128)(2,1)S(1)} %bitcast.34, bf16[1,4096,768]{2,1,0:T(8,128)(2,1)S(1)} %bitcast.41), kind=kOutput, calls=%fused_computation.4 | convolution fusion | flops 6442450944 | bytes 17825792 | tf_op jit(solution)/shard_map/dot_general | solution.py:46
  208.4 0.0 slice-done.2
  208.4 0.0 slice-done.3
  208.4 7.0 %multiply_convert_fusion = bf16[1024,768]{1,0:T(8,128)(2,1)S(1)} fusion(f32[1024,768]{1,0:T(8,128)S(1)} %fusion.2, bf16[1024,4096]{1,0:T(8,128)(2,1)S(1)} %bitcast.35, bf16[1,4096,768]{2,1,0:T(8,128)(2,1)S(1)} %bitcast.43), kind=kOutput, calls=%fused_computation.8 | convolution fusion | flops 6447169536 | bytes 19398656 | tf_op jit(solution)/shard_map/dot_general | solution.py:45
  215.4 13.2 %fusion = f32[16,64,4096]{2,1,0:T(8,128)} fusion(bf16[16,64,768]{2,1,0:T(8,128)(2,1)S(1)} %bitcast.44, bf16[1,768,4096]{2,1,0:T(8,128)(2,1)} %param.17), kind=kOutput, calls=%fused_computation.2 | convolution fusion | flops 6442450944 | bytes 24641536 | tf_op jit(solution)/shard_map/dot_general | solution.py:48
  228.6 0.0 reduce-scatter.2.cloned.1.call-update
  228.6 0.0 copy-start
  228.6 0.0 copy-start.1
  228.6 190.0 %reduce-scatter.2.cloned.1.call-done = f32[16,64,2048]{2,1,0:T(8,128)} async-done(((f32[16,64,4096]{2,1,0:T(8,128)}), f32[16,64,2048]{2,1,0:T(8,128)}) %reduce-scatter.2.cloned.1.call-update) | async-done | bytes 8388624 | tf_op jit(solution)/shard_map/reduce_scatter | solution.py:56
  418.6 6.1 all-to-all-start.1
  424.7 0.0 copy-done
  424.7 0.1 copy.22
  424.8 0.1 copy.23
  424.9 0.1 copy.24
  425.0 0.0 copy-done.1
  425.0 0.5 broadcast_select_fusion
  425.5 181.4 %all-to-all-done.1 = f32[16,64,2048]{2,1,0:T(8,128)} async-done(((f32[16,64,2048]{2,1,0:T(8,128)}), f32[16,64,2048]{2,1,0:T(8,128)}, u32[]{:S(2)}, u32[]{:S(2)}) %all-to-all-start.1) | async-done | bytes 8388640 | tf_op jit(solution)/shard_map/all_to_all | solution.py:57
  606.9 7.6 %fusion.8 = bf16[64,2048]{1,0:T(8,128)(2,1)S(1)} fusion(f32[16,64,2048]{2,1,0:T(8,128)} %all-to-all-done.1, f32[64,16,64]{2,1,0:T(8,128)S(1)} %broadcast_select_fusion), kind=kOutput, calls=%fused_computation.10 | convolution fusion | flops 1610743808 | bytes 8912896 | tf_op jit(solution)/shard_map/dot_general | solution.py:58
  614.6 0.2 reshape.103
  614.8 0.2 convolution_convert_fusion
  615.0 8.3 %all_to_all.26 = bf16[2,8,4,2048]{3,1,2,0:T(8,128)(2,1)S(1)} all-to-all(bf16[2,8,4,2048]{3,1,2,0:T(8,128)(2,1)S(1)} %bitcast.36), channel_id=1, replica_groups=mesh['dp'=2,'expert'=16] {'dp'}, dimensions={0} | all-to-all | bytes 524288 | tf_op jit(solution)/shard_map/all_to_all | solution.py:70
  623.3 0.3 copy.26
  623.6 0.9 reshape.105
  (9 shorter events, 0.1 us)
Async XLA Ops:
  6.5 412.1 %reduce-scatter.2.cloned.1.call-start = ((), (), s32[]{:S(2)}) async-start(), calls=%async_computation.4 | async-start | bytes 25165824 | tf_op jit(solution)/shard_map/reduce_scatter | solution.py:56
  11.0 190.7 %slice-start = ((s8[6291456]{0:T(1024)(128)(4,1)}), s8[4194304]{0:T(1024)(128)(4,1)S(1)}, s32[]{:S(2)}) async-start(s8[6291456]{0:T(1024)(128)(4,1)} %bitcast.40), calls=%async_computation.5 | async-start | bytes 8388608
  13.4 188.3 %slice-start.1 = ((s8[6291456]{0:T(1024)(128)(4,1)}), s8[2097152]{0:T(1024)(128)(4,1)S(1)}, s32[]{:S(2)}) async-start(s8[6291456]{0:T(1024)(128)(4,1)} %bitcast.40), calls=%async_computation.6 | async-start | bytes 4194304
  13.4 195.0 %slice-start.2 = ((s8[6291456]{0:T(1024)(128)(4,1)}), s8[2097152]{0:T(1024)(128)(4,1)S(1)}, s32[]{:S(2)}) async-start(s8[6291456]{0:T(1024)(128)(4,1)} %bitcast.42), calls=%async_computation.7 | async-start | bytes 4194304
  201.8 6.7 %slice-start.3 = ((s8[6291456]{0:T(1024)(128)(4,1)}), s8[4194304]{0:T(1024)(128)(4,1)S(1)}, s32[]{:S(2)}) async-start(s8[6291456]{0:T(1024)(128)(4,1)} %bitcast.42), calls=%async_computation.8 | async-start | bytes 8388608
  228.6 196.1 %copy-start = (f32[16,4,8]{0,2,1:T(8,128)S(1)}, f32[16,4,8]{0,2,1:T(8,128)}, u32[]{:S(2)}) copy-start(f32[16,4,8]{0,2,1:T(8,128)} %param.11) | copy-start | bytes 6148
  228.6 196.4 %copy-start.1 = (s32[16]{0:T(128)S(1)}, s32[16]{0:T(128)}, u32[]{:S(2)}) copy-start(s32[16]{0:T(128)} %param.14) | copy-start | bytes 196
  418.6 188.3 %all-to-all-start.1 = ((f32[16,64,2048]{2,1,0:T(8,128)}), f32[16,64,2048]{2,1,0:T(8,128)}, u32[]{:S(2)}, u32[]{:S(2)}) async-start(f32[16,64,2048]{2,1,0:T(8,128)} %reduce-scatter.2.cloned.1.call-done), calls=%async_computation.2 | async-start | bytes 16777216 | tf_op jit(solution)/shard_map/all_to_all | solution.py:57
Sparse Core Ops, SparseCore 0:
  228.7 189.8 reduce-scatter.1
where the time goes:
time: 632 us; the launch traced here: 631 us
  waiting for transfers between devices  371 us (59%)
  blocking collectives  197 us (31%)
  matrix products  37 us (6%)
  between operations  14.2 us (2%)
    reduce_scatter x1, waiting for transfers between devices, body(): lax.psum_scatter(partial_out, 'dp', scatter_dimension=2, tiled=True)  190 us
    all_to_all x1, blocking collectives, body(): lax.all_to_all(outgoing, 'expert', split_axis=0, concat_axis=0, tiled=True)  188 us
    all_to_all x1, waiting for transfers between devices, body(): lax.all_to_all(columns, 'expert', split_axis=0, concat_axis=0, tiled=True)  181 us
    dot_general x1, matrix products, body(): jnp.dot(activated, w_down[0], preferred_element_type=jnp.float32)  13.2 us
  transfers between devices with their start and end apart: 2, of which 2 were waited for; matrix products, arithmetic and copies ran while one was open for 0% of the time, Pallas kernels for 0%

commit v1 on v0

v1 whole, which is shorter than its diff:
```python
import jax
import jax.numpy as jnp
from jax import lax
from jax.sharding import PartitionSpec as P

CHUNKS = 2


def to_send(kept):
    return kept.astype(jnp.bfloat16)


def fold_bit(value, dim, bit, axis, pairs):
    low = lax.index_in_dim(value, 0, dim, keepdims=False)
    high = lax.index_in_dim(value, 1, dim, keepdims=False)
    kept = jnp.where(bit == 0, low, high)
    sent = jnp.where(bit == 0, high, low)
    arrived = lax.ppermute(sent, axis, pairs)
    return to_send(kept.astype(jnp.float32) + arrived.astype(jnp.float32))


def fold_many(value, count, me, axis, pairs_of):
    total = lax.dynamic_index_in_dim(value, me, 0, keepdims=False).astype(jnp.float32)
    for shift in range(1, count):
        block = lax.dynamic_index_in_dim(value, (me + shift) % count, 0, keepdims=False)
        total = total + lax.ppermute(block, axis, pairs_of(shift)).astype(jnp.float32)
    return to_send(total)


def body(
    hidden_states, routes, route_weight, finish_step, group_keep, dest_slot, w_gate, w_up, w_down
):
    expert_count = lax.axis_size("expert")
    replica_count = lax.axis_size("dp")
    row_count, step_count, model_width = hidden_states.shape
    share_rows = row_count // replica_count
    place = dest_slot // (share_rows * expert_count) * share_rows + dest_slot % share_rows
    order = place[None, :] == lax.broadcasted_iota(jnp.int32, (row_count, row_count), 0)
    step_ids = lax.broadcasted_iota(jnp.int32, (row_count, step_count), 1)
    live = (step_ids < finish_step[:, None]) & (group_keep[0] == 1)
    gate_share = route_weight / jnp.sum(route_weight, axis=2, keepdims=True)
    expert_ids = lax.broadcasted_iota(jnp.int32, (1, 1, 1, expert_count), 3)
    picked = (routes[..., None] == expert_ids) & live[:, :, None, None]
    weight = jnp.sum(jnp.where(picked, gate_share[..., None], 0.0), axis=2)
    weight = jnp.sum(jnp.where(order[:, :, None, None], weight[None], 0.0), axis=1)
    my_expert = lax.axis_index("expert")
    my_replica = lax.axis_index("dp")
    all_weight = lax.all_gather(weight, "expert", axis=0, tiled=False)
    mine = lax.broadcasted_iota(jnp.int32, all_weight.shape, 3) == my_expert
    my_weight = jnp.sum(jnp.where(mine, all_weight, 0.0), axis=3)
    ordered = jnp.dot(
        order.astype(jnp.bfloat16),
        hidden_states.reshape(row_count, step_count * model_width),
        preferred_element_type=jnp.float32,
    ).astype(jnp.bfloat16).reshape(row_count, step_count, model_width)
    part = step_count // CHUNKS
    quad_count = expert_count // 4
    core_bit, side_bit, quad = my_expert % 2, my_expert // 2 % 2, my_expert // 4
    core_pairs = [(e, e ^ 1) for e in range(expert_count)]
    side_pairs = [(e, e ^ 2) for e in range(expert_count)]

    def quad_pairs(shift):
        return [(e, (e + 4 * shift) % expert_count) for e in range(expert_count)]

    def replica_pairs(shift):
        return [(d, (d + shift) % replica_count) for d in range(replica_count)]

    results = []
    for c in range(CHUNKS):
        steps = slice(c * part, (c + 1) * part)
        rows = ordered[:, steps].reshape(replica_count * share_rows * part, model_width)
        gathered = lax.all_gather(rows, "expert", axis=0, tiled=True)
        gate_part = jnp.dot(gathered, w_gate[0], preferred_element_type=jnp.float32)
        up_part = jnp.dot(gathered, w_up[0], preferred_element_type=jnp.float32)
        activated = (jax.nn.silu(gate_part) * up_part).astype(jnp.bfloat16)
        expert_result = jnp.dot(activated, w_down[0], preferred_element_type=jnp.float32)
        scale = my_weight[:, :, steps].reshape(-1, 1)
        partial_out = to_send(expert_result * scale)
        held = partial_out.reshape(
            quad_count, 2, 2, replica_count, share_rows * part, model_width
        )
        held = fold_bit(held, 2, core_bit, "expert", core_pairs)
        half = model_width // 2
        first, second = held[..., :half], held[..., half:]
        first = fold_bit(first, 1, side_bit, "expert", side_pairs)
        first = fold_many(first.swapaxes(0, 1), replica_count, my_replica, "dp", replica_pairs)
        second = fold_many(
            second.transpose(2, 0, 1, 3, 4), replica_count, my_replica, "dp", replica_pairs
        )
        second = fold_bit(second, 1, side_bit, "expert", side_pairs)
        first = fold_many(first, quad_count, quad, "expert", quad_pairs)
        second = fold_many(second, quad_count, quad, "expert", quad_pairs)
        summed = jnp.concatenate([first, second], axis=-1)
        results.append(summed.reshape(share_rows, part, model_width))
    return jnp.concatenate(results, axis=1)


def solution(mesh):
    in_specs = (
        P("expert", None, None),
        P("expert", None, None),
        P("expert", None, None),
        P("expert"),
        P("expert"),
        P("expert"),
        P("expert", None, "dp"),
        P("expert", None, "dp"),
        P("expert", "dp", None),
    )
    out_specs = P(("dp", "expert"), None, None)
    return jax.shard_map(body, mesh=mesh, in_specs=in_specs, out_specs=out_specs, check_vma=False)
```

time: 632 us -> 214 us (0.34)
  waiting for transfers between devices: 371 us -> 80.5 us
  blocking collectives: 197 us -> 17.3 us
  starting transfers between devices: 6.07 us -> 26.3 us
  other arithmetic: 1.76 us -> 14.2 us
  matrix products: 37 us -> 48.1 us
  local copies, waits for them, and re-layouts: 4.21 us -> 11.5 us
    all_to_all x2 -> x0, blocking collectives: 197 us -> none  [the longest x1 188 us: body(): lax.all_to_all(outgoing, 'expert', split_axis=0, concat_axis=0, tiled=True)]
    reduce_scatter x1 -> x0, waiting for transfers between devices: 190 us -> none  [body(): lax.psum_scatter(partial_out, 'dp', scatter_dimension=2, tiled=True)]
    all_to_all x1 -> x0, waiting for transfers between devices: 181 us -> none  [body(): lax.all_to_all(columns, 'expert', split_axis=0, concat_axis=0, tiled=True)]
    all_gather x0 -> x2, waiting for transfers between devices: none -> 53.1 us  [body(): gathered = lax.all_gather(rows, 'expert', axis=0, tiled=True)]
    ppermute x0 -> x22, waiting for transfers between devices: none -> 27.3 us  [the longest x6 15.3 us: fold_bit(): arrived = lax.ppermute(sent, axis, pairs)]
    ppermute x0 -> x22, starting transfers between devices: none -> 26.3 us  [the longest x16 20.5 us: fold_many(): lax.ppermute(block, axis, pairs_of(shift)).astype(jnp.float32)]
    dot_general x1 -> x2, matrix products: 13.2 us -> 33.6 us  [body(): jnp.dot(activated, w_down[0], preferred_element_type=jnp.float32)]
    all_gather x0 -> x1, blocking collectives: none -> 17.3 us  [body(): all_weight = lax.all_gather(weight, 'expert', axis=0, tiled=False)]
  transfers between devices with their start and end apart: 2 -> 24, of which waited for: 2 -> 13; matrix products, arithmetic and copies ran while one was open for 0% -> 32% of each run, Pallas kernels for 0% -> 0%
where the time goes in v1:
time: 214 us; the launch traced here: 212 us
  waiting for transfers between devices  80.5 us (38%)
  matrix products  48.1 us (22%)
  starting transfers between devices  26.3 us (12%)
  blocking collectives  17.3 us (8%)
  between operations  14.5 us (7%)
  other arithmetic  14.2 us (7%)
  local copies, waits for them, and re-layouts  11.5 us (5%)
    all_gather x2, waiting for transfers between devices, body(): gathered = lax.all_gather(rows, 'expert', axis=0, tiled=True)  53.1 us
    dot_general x2, matrix products, body(): jnp.dot(activated, w_down[0], preferred_element_type=jnp.float32)  33.6 us
    ppermute x16, starting transfers between devices, fold_many(): lax.ppermute(block, axis, pairs_of(shift)).astype(jnp.float32)  20.5 us
    all_gather x1, blocking collectives, body(): all_weight = lax.all_gather(weight, 'expert', axis=0, tiled=False)  17.3 us
    ppermute x6, waiting for transfers between devices, fold_bit(): arrived = lax.ppermute(sent, axis, pairs)  15.3 us
    dot_general x2, matrix products, body(): gate_part = jnp.dot(gathered, w_gate[0], preferred_element_type=jnp.float32)  14.3 us
    ppermute x16, waiting for transfers between devices, fold_many(): lax.ppermute(block, axis, pairs_of(shift)).astype(jnp.float32)  12.1 us
    convert_element_type x14, other arithmetic, to_send(): return kept.astype(jnp.bfloat16)  7.73 us
  transfers between devices with their start and end apart: 24, of which 13 were waited for; matrix products, arithmetic and copies ran while one was open for 32% of the time, Pallas kernels for 0%

profile of v1, /device:TPU:10, one launch (start us, length us, event | category | flops | bytes accessed | tf_op | source)
XLA Modules:
  0.0 212.4 jit_solution(8544683753191179288)
XLA Ops:
  6.5 0.7 fusion.46
  7.2 1.3 copy.72
  8.5 0.3 convolution_convert_fusion
  8.9 0.4 reshape.137
  9.2 0.6 fusion.51
  9.8 0.8 reshape.138
  10.7 0.8 reshape.141
  12.5 0.3 select_reduce_fusion.2
  12.8 0.3 select_reduce_fusion.1
  13.2 17.3 %all-gather = f32[256,4,16]{2,1,0:T(4,128)S(1)} all-gather(f32[16,4,16]{2,1,0:T(4,128)S(1)} %select_reduce_fusion.1), channel_id=2, replica_groups=mesh['dp'=2,'expert'=16] {'expert'}, dimensions={0}, use_global_device_ids=true | all-gather | bytes 69632 | tf_op jit(solution)/shard_map/all_gather | solution.py:48
  30.5 0.3 select_reduce_fusion
  30.9 0.1 mul.39
  31.1 0.1 mul.44
  31.2 31.5 %all-gather.4.cloned.1.call-done = bf16[512,4096]{1,0:T(8,128)(2,1)} async-done(((bf16[32,4096]{1,0:T(8,128)(2,1)}), bf16[512,4096]{1,0:T(8,128)(2,1)}) %all-gather.4.cloned.1.call-update) | async-done | bytes 4194320 | tf_op jit(solution)/shard_map/all_gather | solution.py:72
  62.8 7.0 %fusion.8 = f32[512,768]{1,0:T(8,128)S(1)} fusion(bf16[512,4096]{1,0:T(8,128)(2,1)} %all-gather.4.cloned.1.call-done, bf16[1,4096,768]{2,1,0:T(8,128)(2,1)} %param.15), kind=kOutput, calls=%fused_computation.11 | convolution fusion | flops 3221225472 | bytes 12058624 | tf_op jit(solution)/shard_map/dot_general | solution.py:73
  69.8 16.9 %multiply_convert_fusion.1 = bf16[512,4096]{1,0:T(8,128)(2,1)} fusion(bf16[1,768,4096]{2,1,0:T(8,128)(2,1)} %param.17, f32[512]{0:T(512)S(1)} %mul.39, f32[512,768]{1,0:T(8,128)S(1)} %fusion.8, bf16[512,4096]{1,0:T(8,128)(2,1)} %all-gather.4.cloned.1.call-done, bf16[1,4096,768]{2,1,0:T(8,128)(2,1)} %param.16), kind=kOutput, calls=%fused_computation.2 | convolution fusion | flops 6449004544 | bytes 22546432 | tf_op jit(solution)/shard_map/dot_general | solution.py:76
  86.7 2.7 %fusion.49 = (bf16[4,2,1,2,16,4096]{5,4,3,2,1,0:T(8,128)(2,1)S(1)}, bf16[4,2,1,2,16,4096]{5,4,3,2,1,0:T(8,128)(2,1)S(1)}) fusion(bf16[4,2,2,2,16,4096]{5,4,3,2,1,0:T(8,128)(2,1)} %bitcast.150), kind=kLoop, calls=%fused_computation.101 | loop fusion | bytes 8388608 | tf_op jit(solution)/shard_map/slice | solution.py:14
  89.5 1.7 select_bitcast_fusion.1
  91.1 0.3 copy-done.2
  91.4 0.7 copy-done.3
  92.1 0.3 collective-permute-start
  92.4 21.6 %all-gather.6.cloned.1.call-done = bf16[512,4096]{1,0:T(8,128)(2,1)} async-done(((bf16[32,4096]{1,0:T(8,128)(2,1)}), bf16[512,4096]{1,0:T(8,128)(2,1)}) %all-gather.6.cloned.1.call-update) | async-done | bytes 4194320 | tf_op jit(solution)/shard_map/all_gather | solution.py:72
  114.0 7.3 %fusion.6 = f32[512,768]{1,0:T(8,128)S(1)} fusion(bf16[512,4096]{1,0:T(8,128)(2,1)} %all-gather.6.cloned.1.call-done, bf16[1,4096,768]{2,1,0:T(8,128)(2,1)} %param.15), kind=kOutput, calls=%fused_computation.9 | convolution fusion | flops 3221225472 | bytes 12058624 | tf_op jit(solution)/shard_map/dot_general | solution.py:73
  121.3 16.7 %multiply_convert_fusion = bf16[512,4096]{1,0:T(8,128)(2,1)} fusion(bf16[1,768,4096]{2,1,0:T(8,128)(2,1)} %param.17, f32[512]{0:T(512)S(1)} %mul.44, f32[512,768]{1,0:T(8,128)S(1)} %fusion.6, bf16[512,4096]{1,0:T(8,128)(2,1)} %all-gather.6.cloned.1.call-done, bf16[1,4096,768]{2,1,0:T(8,128)(2,1)} %param.16), kind=kOutput, calls=%fused_computation.1 | convolution fusion | flops 6449004544 | bytes 22546432 | tf_op jit(solution)/shard_map/dot_general | solution.py:76
  137.9 2.6 %fusion.50 = (bf16[4,2,1,2,16,4096]{5,4,3,2,1,0:T(8,128)(2,1)S(1)}, bf16[4,2,1,2,16,4096]{5,4,3,2,1,0:T(8,128)(2,1)S(1)}) fusion(bf16[4,2,2,2,16,4096]{5,4,3,2,1,0:T(8,128)(2,1)} %bitcast.151), kind=kLoop, calls=%fused_computation.102 | loop fusion | bytes 8388608 | tf_op jit(solution)/shard_map/slice | solution.py:14
  140.5 1.8 select_bitcast_fusion
  142.4 0.1 copy-done
  142.5 0.3 collective-permute-start.11
  142.8 3.9 %fusion.11 = bf16[4,2,2,16,4096]{4,3,0,1,2:T(8,128)(2,1)S(1)} fusion(bf16[4,2,2,16,4096]{4,3,0,1,2:T(8,128)(2,1)} %collective-permute-done, pred[]{:T(512)S(6)} %eq.76, bf16[4,2,1,2,16,4096]{5,4,3,2,1,0:T(8,128)(2,1)} %copy-done.3, bf16[4,2,1,2,16,4096]{5,4,3,2,1,0:T(8,128)(2,1)} %copy-done.2), kind=kLoop, calls=%fused_computation.16 | loop fusion | flops 5242880 | bytes 8388609 | tf_op jit(solution)/shard_map/convert_element_type | solution.py:10
  146.8 1.5 collective-permute-start.1
  148.4 1.5 collective-permute-start.6
  150.0 2.6 %fusion.10 = bf16[4,2,2,16,4096]{4,3,0,1,2:T(8,128)(2,1)S(1)} fusion(bf16[4,2,2,16,4096]{4,3,0,1,2:T(8,128)(2,1)} %collective-permute-done.11, pred[]{:T(512)S(6)} %eq.76, bf16[4,2,1,2,16,4096]{5,4,3,2,1,0:T(8,128)(2,1)S(1)} %copy-done.1, bf16[4,2,1,2,16,4096]{5,4,3,2,1,0:T(8,128)(2,1)S(1)} %get-tuple-element.7), kind=kLoop, calls=%fused_computation.14 | loop fusion | flops 5242880 | bytes 8388609 | tf_op jit(solution)/shard_map/convert_element_type | solution.py:10
  152.7 0.6 collective-permute-start.12
  153.4 0.7 collective-permute-start.17
  154.1 7.5 %collective-permute-done.1 = bf16[4,2,16,2048]{3,2,0,1:T(8,128)(2,1)S(1)} collective-permute-done((bf16[4,2,16,2048]{3,2,0,1:T(8,128)(2,1)S(1)}, bf16[4,2,16,2048]{3,2,0,1:T(8,128)(2,1)S(1)}, u32[]{:S(2)}, u32[]{:S(2)}) %collective-permute-start.1) | collective-permute-done | bytes 524320 | tf_op jit(solution)/shard_map/ppermute | solution.py:18
  161.7 0.2 fusion.19
  161.9 1.5 collective-permute-start.2
  163.5 0.1 fusion.18
  163.7 1.5 collective-permute-start.7
  165.2 7.7 %collective-permute-done.12 = bf16[4,2,16,2048]{3,2,0,1:T(8,128)(2,1)S(1)} collective-permute-done((bf16[4,2,16,2048]{3,2,0,1:T(8,128)(2,1)S(1)}, bf16[4,2,16,2048]{3,2,0,1:T(8,128)(2,1)S(1)}, u32[]{:S(2)}, u32[]{:S(2)}) %collective-permute-start.12) | collective-permute-done | bytes 524320 | tf_op jit(solution)/shard_map/ppermute | solution.py:18
  172.9 0.2 fusion.17
  173.2 1.5 collective-permute-start.13
  174.7 0.1 fusion.16
  174.9 1.5 collective-permute-start.18
  176.4 3.7 %collective-permute-done.2 = bf16[4,16,2048]{2,1,0:T(8,128)(2,1)S(1)} collective-permute-done((bf16[4,16,2048]{2,1,0:T(8,128)(2,1)S(1)}, bf16[4,16,2048]{2,1,0:T(8,128)(2,1)S(1)}, u32[]{:S(2)}, u32[]{:S(2)}) %collective-permute-start.2) | collective-permute-done | bytes 262176 | tf_op jit(solution)/shard_map/ppermute | solution.py:26
  180.2 0.9 collective-permute-start.3
  181.1 2.0 collective-permute-start.4
  183.3 1.4 collective-permute-done.13
  184.7 1.0 collective-permute-start.10
  185.8 1.1 collective-permute-start.8
  187.1 2.8 %collective-permute-start.9 = (bf16[16,2048]{1,0:T(8,128)(2,1)S(1)}, bf16[16,2048]{1,0:T(8,128)(2,1)S(1)}, u32[]{:S(2)}, u32[]{:S(2)}) collective-permute-start(bf16[16,2048]{1,0:T(8,128)(2,1)S(1)} %get-tuple-element.16), channel_id=1, source_target_pairs={{0,8},{1,9},{2,10},{3,11},{4,12},{5,13},{6,14},{7,15},{8,0},{9,1},... | collective-permute-start | bytes 196616 | tf_op jit(solution)/shard_map/ppermute | solution.py:26
  189.9 2.0 collective-permute-start.15
  191.9 2.0 collective-permute-done.10
  193.9 2.0 collective-permute-start.19
  195.9 1.9 collective-permute-start.20
  197.9 0.4 collective-permute-done.14
  198.2 1.5 collective-permute-start.21
  199.8 2.5 %collective-permute-done.16 = bf16[16,2048]{1,0:T(8,128)(2,1)S(1)} collective-permute-done((bf16[16,2048]{1,0:T(8,128)(2,1)S(1)}, bf16[16,2048]{1,0:T(8,128)(2,1)S(1)}, u32[]{:S(2)}, u32[]{:S(2)}) %collective-permute-start.16) | collective-permute-done | bytes 65568 | tf_op jit(solution)/shard_map/ppermute | solution.py:26
  202.4 0.1 reshape.140
  202.5 0.1 collective-permute-done.19
  202.6 0.7 collective-permute-done.20
  203.3 1.1 collective-permute-done.21
  204.5 0.1 reshape.143
  204.6 1.0 pad_maximum_fusion
  (62 shorter events, 1.7 us)
Async XLA Ops:
  6.5 56.2 %all-gather.4.cloned.1.call-start = ((), (), s32[]{:S(2)}) async-start(), calls=%async_computation | async-start | bytes 4456448 | tf_op jit(solution)/shard_map/all_gather | solution.py:72
  8.8 2.7 %copy-start.4 = (f32[16,4,8]{0,2,1:T(8,128)S(1)}, f32[16,4,8]{0,2,1:T(8,128)}, u32[]{:S(2)}) copy-start(f32[16,4,8]{0,2,1:T(8,128)} %param.11) | copy-start | bytes 6148
  8.8 2.8 %copy-start.5 = (s32[16,4,8]{0,2,1:T(8,128)S(1)}, s32[16,4,8]{0,2,1:T(8,128)}, u32[]{:S(2)}) copy-start(s32[16,4,8]{0,2,1:T(8,128)} %param.10) | copy-start | bytes 6148
  8.8 3.6 %copy-start.6 = (s32[16]{0:T(128)S(1)}, s32[16]{0:T(128)}, u32[]{:S(2)}) copy-start(s32[16]{0:T(128)} %param.12) | copy-start | bytes 196
  10.7 103.4 %all-gather.6.cloned.1.call-start = ((), (), s32[]{:S(2)}) async-start(), calls=%async_computation.1 | async-start | bytes 4456448 | tf_op jit(solution)/shard_map/all_gather | solution.py:72
  89.4 2.0 copy-start.2
  89.4 2.7 %copy-start.3 = (bf16[4,2,1,2,16,4096]{5,4,3,2,1,0:T(8,128)(2,1)}, bf16[4,2,1,2,16,4096]{5,4,3,2,1,0:T(8,128)(2,1)S(1)}, u32[]{:S(2)}) copy-start(bf16[4,2,1,2,16,4096]{5,4,3,2,1,0:T(8,128)(2,1)S(1)} %get-tuple-element.6) | copy-start | bytes 6291460
  92.1 50.6 %collective-permute-start = (bf16[4,2,2,16,4096]{4,3,0,1,2:T(8,128)(2,1)}, bf16[4,2,2,16,4096]{4,3,0,1,2:T(8,128)(2,1)}, u32[]{:S(2)}, u32[]{:S(2)}) collective-permute-start(bf16[4,2,2,16,4096]{4,3,0,1,2:T(8,128)(2,1)} %select_bitcast_fusion.1), channel_id=1, source_target_pairs={{0,1},{1,0},{2,3},{3,2},{4,5},{5,4},{6,7},{7,6},{8,9},{9,8},{10,11... | collective-permute-start | bytes 6291464 | tf_op jit(solution)/shard_map/ppermute | solution.py:18
  140.5 2.0 copy-start
  142.5 7.5 %collective-permute-start.11 = (bf16[4,2,2,16,4096]{4,3,0,1,2:T(8,128)(2,1)}, bf16[4,2,2,16,4096]{4,3,0,1,2:T(8,128)(2,1)}, u32[]{:S(2)}, u32[]{:S(2)}) collective-permute-start(bf16[4,2,2,16,4096]{4,3,0,1,2:T(8,128)(2,1)} %select_bitcast_fusion), channel_id=1, source_target_pairs={{0,1},{1,0},{2,3},{3,2},{4,5},{5,4},{6,7},{7,6},{8,9},{9,8},{10,11... | collective-permute-start | bytes 6291464 | tf_op jit(solution)/shard_map/ppermute | solution.py:18
  146.7 3.3 %copy-start.1 = (bf16[4,2,1,2,16,4096]{5,4,3,2,1,0:T(8,128)(2,1)S(1)}, bf16[4,2,1,2,16,4096]{5,4,3,2,1,0:T(8,128)(2,1)}, u32[]{:S(2)}) copy-start(bf16[4,2,1,2,16,4096]{5,4,3,2,1,0:T(8,128)(2,1)} %copy-done) | copy-start | bytes 6291460
  146.8 14.8 %collective-permute-start.1 = (bf16[4,2,16,2048]{3,2,0,1:T(8,128)(2,1)S(1)}, bf16[4,2,16,2048]{3,2,0,1:T(8,128)(2,1)S(1)}, u32[]{:S(2)}, u32[]{:S(2)}) collective-permute-start(bf16[4,2,16,2048]{3,2,0,1:T(8,128)(2,1)S(1)} %fusion.31), channel_id=1, source_target_pairs={{0,2},{1,3},{2,0},{3,1},{4,6},{5,7},{6,4},{7,5},{8,10},{9,11},{10,... | collective-permute-start | bytes 1572872 | tf_op jit(solution)/shard_map/ppermute | solution.py:18
  148.4 15.1 %collective-permute-start.6 = (bf16[4,2,16,2048]{3,2,0,1:T(8,128)(2,1)S(1)}, bf16[4,2,16,2048]{3,2,0,1:T(8,128)(2,1)S(1)}, u32[]{:S(2)}, u32[]{:S(2)}) collective-permute-start(bf16[4,2,16,2048]{3,2,0,1:T(8,128)(2,1)S(1)} %dynamic-slice_bitcast_fusion.1), channel_id=1, source_target_pairs={{0,16},{16,0},{1,17},{17,1},{2,18},{18,2},{3,19},{19,3},{4,20},{20... | collective-permute-start | bytes 1572872 | tf_op jit(solution)/shard_map/ppermute | solution.py:26
  152.7 20.2 %collective-permute-start.12 = (bf16[4,2,16,2048]{3,2,0,1:T(8,128)(2,1)S(1)}, bf16[4,2,16,2048]{3,2,0,1:T(8,128)(2,1)S(1)}, u32[]{:S(2)}, u32[]{:S(2)}) collective-permute-start(bf16[4,2,16,2048]{3,2,0,1:T(8,128)(2,1)S(1)} %fusion.25), channel_id=1, source_target_pairs={{0,2},{1,3},{2,0},{3,1},{4,6},{5,7},{6,4},{7,5},{8,10},{9,11},{10,... | collective-permute-start | bytes 1572872 | tf_op jit(solution)/shard_map/ppermute | solution.py:18
  153.4 21.3 %collective-permute-start.17 = (bf16[4,2,16,2048]{3,2,0,1:T(8,128)(2,1)S(1)}, bf16[4,2,16,2048]{3,2,0,1:T(8,128)(2,1)S(1)}, u32[]{:S(2)}, u32[]{:S(2)}) collective-permute-start(bf16[4,2,16,2048]{3,2,0,1:T(8,128)(2,1)S(1)} %dynamic-slice_bitcast_fusion), channel_id=1, source_target_pairs={{0,16},{16,0},{1,17},{17,1},{2,18},{18,2},{3,19},{19,3},{4,20},{20... | collective-permute-start | bytes 1572872 | tf_op jit(solution)/shard_map/ppermute | solution.py:26
  161.9 18.2 %collective-permute-start.2 = (bf16[4,16,2048]{2,1,0:T(8,128)(2,1)S(1)}, bf16[4,16,2048]{2,1,0:T(8,128)(2,1)S(1)}, u32[]{:S(2)}, u32[]{:S(2)}) collective-permute-start(bf16[4,16,2048]{2,1,0:T(8,128)(2,1)S(1)} %dynamic-slice_bitcast_fusion.3), channel_id=1, source_target_pairs={{0,16},{16,0},{1,17},{17,1},{2,18},{18,2},{3,19},{19,3},{4,20},{20... | collective-permute-start | bytes 786440 | tf_op jit(solution)/shard_map/ppermute | solution.py:26
  163.7 19.5 %collective-permute-start.7 = (bf16[4,16,2048]{2,1,0:T(8,128)(2,1)S(1)}, bf16[4,16,2048]{2,1,0:T(8,128)(2,1)S(1)}, u32[]{:S(2)}, u32[]{:S(2)}) collective-permute-start(bf16[4,16,2048]{2,1,0:T(8,128)(2,1)S(1)} %select_bitcast_fusion.3), channel_id=1, source_target_pairs={{0,2},{1,3},{2,0},{3,1},{4,6},{5,7},{6,4},{7,5},{8,10},{9,11},{10,... | collective-permute-start | bytes 786440 | tf_op jit(solution)/shard_map/ppermute | solution.py:18
  173.2 11.6 %collective-permute-start.13 = (bf16[4,16,2048]{2,1,0:T(8,128)(2,1)S(1)}, bf16[4,16,2048]{2,1,0:T(8,128)(2,1)S(1)}, u32[]{:S(2)}, u32[]{:S(2)}) collective-permute-start(bf16[4,16,2048]{2,1,0:T(8,128)(2,1)S(1)} %dynamic-slice_bitcast_fusion.2), channel_id=1, source_target_pairs={{0,16},{16,0},{1,17},{17,1},{2,18},{18,2},{3,19},{19,3},{4,20},{20... | collective-permute-start | bytes 786440 | tf_op jit(solution)/shard_map/ppermute | solution.py:26
  174.9 10.9 %collective-permute-start.18 = (bf16[4,16,2048]{2,1,0:T(8,128)(2,1)S(1)}, bf16[4,16,2048]{2,1,0:T(8,128)(2,1)S(1)}, u32[]{:S(2)}, u32[]{:S(2)}) collective-permute-start(bf16[4,16,2048]{2,1,0:T(8,128)(2,1)S(1)} %select_bitcast_fusion.2), channel_id=1, source_target_pairs={{0,2},{1,3},{2,0},{3,1},{4,6},{5,7},{6,4},{7,5},{8,10},{9,11},{10,... | collective-permute-start | bytes 786440 | tf_op jit(solution)/shard_map/ppermute | solution.py:18
  180.2 6.8 %collective-permute-start.3 = (bf16[16,2048]{1,0:T(8,128)(2,1)S(1)}, bf16[16,2048]{1,0:T(8,128)(2,1)S(1)}, u32[]{:S(2)}, u32[]{:S(2)}) collective-permute-start(bf16[16,2048]{1,0:T(8,128)(2,1)S(1)} %get-tuple-element.11), channel_id=1, source_target_pairs={{0,4},{1,5},{2,6},{3,7},{4,8},{5,9},{6,10},{7,11},{8,12},{9,13},{1... | collective-permute-start | bytes 196616 | tf_op jit(solution)/shard_map/ppermute | solution.py:26
  181.1 8.7 %collective-permute-start.4 = (bf16[16,2048]{1,0:T(8,128)(2,1)S(1)}, bf16[16,2048]{1,0:T(8,128)(2,1)S(1)}, u32[]{:S(2)}, u32[]{:S(2)}) collective-permute-start(bf16[16,2048]{1,0:T(8,128)(2,1)S(1)} %get-tuple-element.13), channel_id=1, source_target_pairs={{0,8},{1,9},{2,10},{3,11},{4,12},{5,13},{6,14},{7,15},{8,0},{9,1},... | collective-permute-start | bytes 196616 | tf_op jit(solution)/shard_map/ppermute | solution.py:26
  183.2 6.7 %collective-permute-start.5 = (bf16[16,2048]{1,0:T(8,128)(2,1)S(1)}, bf16[16,2048]{1,0:T(8,128)(2,1)S(1)}, u32[]{:S(2)}, u32[]{:S(2)}) collective-permute-start(bf16[16,2048]{1,0:T(8,128)(2,1)S(1)} %get-tuple-element.12), channel_id=1, source_target_pairs={{0,12},{1,13},{2,14},{3,15},{4,0},{5,1},{6,2},{7,3},{8,4},{9,5},{1... | collective-permute-start | bytes 196616 | tf_op jit(solution)/shard_map/ppermute | solution.py:26
  184.7 9.2 %collective-permute-start.10 = (bf16[16,2048]{1,0:T(8,128)(2,1)S(1)}, bf16[16,2048]{1,0:T(8,128)(2,1)S(1)}, u32[]{:S(2)}, u32[]{:S(2)}) collective-permute-start(bf16[16,2048]{1,0:T(8,128)(2,1)S(1)} %get-tuple-element.15), channel_id=1, source_target_pairs={{0,12},{1,13},{2,14},{3,15},{4,0},{5,1},{6,2},{7,3},{8,4},{9,5},{1... | collective-permute-start | bytes 196616 | tf_op jit(solution)/shard_map/ppermute | solution.py:26
  185.8 8.1 %collective-permute-start.8 = (bf16[16,2048]{1,0:T(8,128)(2,1)S(1)}, bf16[16,2048]{1,0:T(8,128)(2,1)S(1)}, u32[]{:S(2)}, u32[]{:S(2)}) collective-permute-start(bf16[16,2048]{1,0:T(8,128)(2,1)S(1)} %get-tuple-element.14), channel_id=1, source_target_pairs={{0,4},{1,5},{2,6},{3,7},{4,8},{5,9},{6,10},{7,11},{8,12},{9,13},{1... | collective-permute-start | bytes 196616 | tf_op jit(solution)/shard_map/ppermute | solution.py:26
  187.1 8.9 %collective-permute-start.9 = (bf16[16,2048]{1,0:T(8,128)(2,1)S(1)}, bf16[16,2048]{1,0:T(8,128)(2,1)S(1)}, u32[]{:S(2)}, u32[]{:S(2)}) collective-permute-start(bf16[16,2048]{1,0:T(8,128)(2,1)S(1)} %get-tuple-element.16), channel_id=1, source_target_pairs={{0,8},{1,9},{2,10},{3,11},{4,12},{5,13},{6,14},{7,15},{8,0},{9,1},... | collective-permute-start | bytes 196616 | tf_op jit(solution)/shard_map/ppermute | solution.py:26
  189.8 8.4 %collective-permute-start.14 = (bf16[16,2048]{1,0:T(8,128)(2,1)S(1)}, bf16[16,2048]{1,0:T(8,128)(2,1)S(1)}, u32[]{:S(2)}, u32[]{:S(2)}) collective-permute-start(bf16[16,2048]{1,0:T(8,128)(2,1)S(1)} %get-tuple-element.17), channel_id=1, source_target_pairs={{0,4},{1,5},{2,6},{3,7},{4,8},{5,9},{6,10},{7,11},{8,12},{9,13},{1... | collective-permute-start | bytes 196616 | tf_op jit(solution)/shard_map/ppermute | solution.py:26
  189.9 9.9 %collective-permute-start.15 = (bf16[16,2048]{1,0:T(8,128)(2,1)S(1)}, bf16[16,2048]{1,0:T(8,128)(2,1)S(1)}, u32[]{:S(2)}, u32[]{:S(2)}) collective-permute-start(bf16[16,2048]{1,0:T(8,128)(2,1)S(1)} %get-tuple-element.19), channel_id=1, source_target_pairs={{0,8},{1,9},{2,10},{3,11},{4,12},{5,13},{6,14},{7,15},{8,0},{9,1},... | collective-permute-start | bytes 196616 | tf_op jit(solution)/shard_map/ppermute | solution.py:26
  193.9 8.4 %collective-permute-start.16 = (bf16[16,2048]{1,0:T(8,128)(2,1)S(1)}, bf16[16,2048]{1,0:T(8,128)(2,1)S(1)}, u32[]{:S(2)}, u32[]{:S(2)}) collective-permute-start(bf16[16,2048]{1,0:T(8,128)(2,1)S(1)} %get-tuple-element.18), channel_id=1, source_target_pairs={{0,12},{1,13},{2,14},{3,15},{4,0},{5,1},{6,2},{7,3},{8,4},{9,5},{1... | collective-permute-start | bytes 196616 | tf_op jit(solution)/shard_map/ppermute | solution.py:26
  193.9 8.7 %collective-permute-start.19 = (bf16[16,2048]{1,0:T(8,128)(2,1)S(1)}, bf16[16,2048]{1,0:T(8,128)(2,1)S(1)}, u32[]{:S(2)}, u32[]{:S(2)}) collective-permute-start(bf16[16,2048]{1,0:T(8,128)(2,1)S(1)} %get-tuple-element.20), channel_id=1, source_target_pairs={{0,4},{1,5},{2,6},{3,7},{4,8},{5,9},{6,10},{7,11},{8,12},{9,13},{1... | collective-permute-start | bytes 196616 | tf_op jit(solution)/shard_map/ppermute | solution.py:26
  195.9 7.4 %collective-permute-start.20 = (bf16[16,2048]{1,0:T(8,128)(2,1)S(1)}, bf16[16,2048]{1,0:T(8,128)(2,1)S(1)}, u32[]{:S(2)}, u32[]{:S(2)}) collective-permute-start(bf16[16,2048]{1,0:T(8,128)(2,1)S(1)} %get-tuple-element.22), channel_id=1, source_target_pairs={{0,8},{1,9},{2,10},{3,11},{4,12},{5,13},{6,14},{7,15},{8,0},{9,1},... | collective-permute-start | bytes 196616 | tf_op jit(solution)/shard_map/ppermute | solution.py:26
  198.2 6.2 %collective-permute-start.21 = (bf16[16,2048]{1,0:T(8,128)(2,1)S(1)}, bf16[16,2048]{1,0:T(8,128)(2,1)S(1)}, u32[]{:S(2)}, u32[]{:S(2)}) collective-permute-start(bf16[16,2048]{1,0:T(8,128)(2,1)S(1)} %get-tuple-element.21), channel_id=1, source_target_pairs={{0,12},{1,13},{2,14},{3,15},{4,0},{5,1},{6,2},{7,3},{8,4},{9,5},{1... | collective-permute-start | bytes 196616 | tf_op jit(solution)/shard_map/ppermute | solution.py:26
Sparse Core Ops, SparseCore 0:
  10.8 51.9 all-gather.3
  64.9 49.0 all-gather.5

commit v2 on v1

v2 whole, which is shorter than its diff:
```python
import jax
import jax.numpy as jnp
from jax import lax
from jax.sharding import PartitionSpec as P

CHUNKS = 2


def to_send(kept):
    return kept.astype(jnp.bfloat16)


def added(*terms):
    total = terms[0].astype(jnp.float32)
    for term in terms[1:]:
        total = total + term.astype(jnp.float32)
    return to_send(total)


def spread(value, axis, peers):
    return jnp.stack([value] + [lax.ppermute(value, axis, [(b, a) for a, b in p]) for p in peers])


def fold(value, axis, peers):
    return added(value[0], *[lax.ppermute(value[r + 1], axis, p) for r, p in enumerate(peers)])


def body(
    hidden_states, routes, route_weight, finish_step, group_keep, dest_slot, w_gate, w_up, w_down
):
    expert_count = lax.axis_size("expert")
    replica_count = lax.axis_size("dp")
    row_count, step_count, model_width = hidden_states.shape
    share_rows = row_count // replica_count
    place = dest_slot // (share_rows * expert_count) * share_rows + dest_slot % share_rows
    order = place[None, :] == lax.broadcasted_iota(jnp.int32, (row_count, row_count), 0)
    step_ids = lax.broadcasted_iota(jnp.int32, (row_count, step_count), 1)
    live = (step_ids < finish_step[:, None]) & (group_keep[0] == 1)
    gate_share = route_weight / jnp.sum(route_weight, axis=2, keepdims=True)
    expert_ids = lax.broadcasted_iota(jnp.int32, (1, 1, 1, expert_count), 3)
    picked = (routes[..., None] == expert_ids) & live[:, :, None, None]
    weight = jnp.sum(jnp.where(picked, gate_share[..., None], 0.0), axis=2)
    weight = jnp.sum(jnp.where(order[:, :, None, None], weight[None], 0.0), axis=1)
    my_expert = lax.axis_index("expert")
    my_replica = lax.axis_index("dp")
    all_weight = lax.all_gather(weight, "expert", axis=0, tiled=False)
    mine = lax.broadcasted_iota(jnp.int32, all_weight.shape, 3) == my_expert
    my_weight = jnp.sum(jnp.where(mine, all_weight, 0.0), axis=3)
    ordered = jnp.dot(
        order.astype(jnp.bfloat16),
        hidden_states.reshape(row_count, step_count * model_width),
        preferred_element_type=jnp.float32,
    ).astype(jnp.bfloat16).reshape(row_count, step_count, model_width)
    part = step_count // CHUNKS
    block = share_rows * part
    quad_count = expert_count // 4
    core_peers = [[(e, e ^ 1) for e in range(expert_count)]]
    side_peers = [[(e, e ^ 2) for e in range(expert_count)]]
    quad_peers = [
        [(e, (e + 4 * r) % expert_count) for e in range(expert_count)] for r in range(1, quad_count)
    ]
    dp_peers = [
        [(d, (d + r) % replica_count) for d in range(replica_count)] for r in range(1, replica_count)
    ]
    shape = (2, replica_count, 2, quad_count)
    away = [lax.broadcasted_iota(jnp.int32, shape, k) for k in range(4)]
    owner_expert = (my_expert // 4 + away[3]) % quad_count * 4
    owner_expert += (my_expert // 2 + away[2]) % 2 * 2 + (my_expert + away[0]) % 2
    owner = owner_expert * replica_count + (my_replica + away[1]) % replica_count
    owner = owner.reshape(-1, 1)
    blocks = expert_count * replica_count
    wanted = owner == lax.broadcasted_iota(jnp.int32, (blocks, blocks), 1)
    by_owner = my_weight.reshape(1, blocks, share_rows * step_count)
    my_weight = jnp.sum(jnp.where(wanted[:, :, None], by_owner, 0.0), axis=1)
    my_weight = my_weight.reshape(blocks, share_rows, step_count)
    own = ordered.reshape(replica_count, share_rows, step_count, model_width)
    own = lax.dynamic_index_in_dim(own, my_replica, 0, keepdims=False)
    half = model_width // 2
    results = []
    for c in range(CHUNKS):
        steps = slice(c * part, (c + 1) * part)
        line = spread(own[:, steps].reshape(block, model_width), "expert", quad_peers)
        first = spread(spread(line[..., :half], "expert", side_peers), "dp", dp_peers)
        second = spread(spread(line[..., half:], "dp", dp_peers), "expert", side_peers)
        plane = jnp.concatenate([first, second.swapaxes(0, 1)], axis=-1)
        gathered = spread(plane, "expert", core_peers).reshape(blocks * block, model_width)
        gate_part = jnp.dot(gathered, w_gate[0], preferred_element_type=jnp.float32)
        up_part = jnp.dot(gathered, w_up[0], preferred_element_type=jnp.float32)
        activated = (jax.nn.silu(gate_part) * up_part).astype(jnp.bfloat16)
        expert_result = jnp.dot(activated, w_down[0], preferred_element_type=jnp.float32)
        partial_out = to_send(expert_result * my_weight[:, :, steps].reshape(-1, 1))
        held = partial_out.reshape(shape + (block, model_width))
        held = fold(held, "expert", core_peers)
        first, second = held[..., :half], held[..., half:].swapaxes(0, 1)
        first = fold(first.swapaxes(0, 1), "expert", side_peers)
        second = fold(second.swapaxes(0, 1), "dp", dp_peers)
        first = fold(first, "dp", dp_peers)
        second = fold(second, "expert", side_peers)
        first = fold(first, "expert", quad_peers)
        second = fold(second, "expert", quad_peers)
        summed = jnp.concatenate([first, second], axis=-1)
        results.append(summed.reshape(share_rows, part, model_width))
    return jnp.concatenate(results, axis=1)


def solution(mesh):
    in_specs = (
        P("expert", None, None),
        P("expert", None, None),
        P("expert", None, None),
        P("expert"),
        P("expert"),
        P("expert"),
        P("expert", None, "dp"),
        P("expert", None, "dp"),
        P("expert", "dp", None),
    )
    out_specs = P(("dp", "expert"), None, None)
    return jax.shard_map(body, mesh=mesh, in_specs=in_specs, out_specs=out_specs, check_vma=False)
```

time: 214 us -> 217 us (1.014)
  starting transfers between devices: 26.3 us -> 42.1 us
  between operations: 14.5 us -> 1.36 us
  waiting for transfers between devices: 80.5 us -> 71.1 us
  other arithmetic: 14.2 us -> 22.2 us
  local copies, waits for them, and re-layouts: 11.5 us -> 17.6 us
  matrix products: 48.1 us -> 42.1 us
    all_gather x2 -> x0, waiting for transfers between devices: 53.1 us -> none  [body(): gathered = lax.all_gather(rows, 'expert', axis=0, tiled=True)]
    ppermute x22 -> x38, waiting for transfers between devices: 27.3 us -> 71.1 us  [the longest x16 40.5 us: spread(): lax.ppermute(value, axis, [(b, a) for a, b in p])]
    ppermute x22 -> x38, starting transfers between devices: 26.3 us -> 42.1 us  [the longest x22 27.2 us: fold(): lax.ppermute(value[r + 1], axis, p)]
    another operation x0 -> x10, other arithmetic: none -> 13.8 us  [spread(): jnp.stack([value] + [lax.ppermute(value, axis, [(b, a) for a, b in p]) fo...]
    dot_general x2, matrix products: 14.3 us -> 8.03 us  [body(): gate_part = jnp.dot(gathered, w_gate[0], preferred_element_type=jnp.float32)]
    select_n x6 -> x0, other arithmetic: 3.68 us -> none  [fold_bit(): sent = jnp.where(bit == 0, high, low)]
    convert_element_type x14, other arithmetic: 7.73 us -> 4.06 us  [to_send(): return kept.astype(jnp.bfloat16)]
    unnamed x16 -> x24, local copies, waits for them, and re-layouts: 2.56 us -> 6.14 us
  transfers between devices with their start and end apart: 24 -> 38, of which waited for: 13 -> 16; matrix products, arithmetic and copies ran while one was open for 32% -> 33% of each run, Pallas kernels for 0% -> 0%
where the time goes in v2:
time: 217 us; the launch traced here: 215 us
  waiting for transfers between devices  71.1 us (33%)
  matrix products  42.1 us (19%)
  starting transfers between devices  42.1 us (19%)
  other arithmetic  22.2 us (10%)
  blocking collectives  18.1 us (8%)
  local copies, waits for them, and re-layouts  17.6 us (8%)
    ppermute x16, waiting for transfers between devices, spread(): lax.ppermute(value, axis, [(b, a) for a, b in p])  40.5 us
    dot_general x2, matrix products, body(): jnp.dot(activated, w_down[0], preferred_element_type=jnp.float32)  33.8 us
    ppermute x22, waiting for transfers between devices, fold(): lax.ppermute(value[r + 1], axis, p)  30.7 us
    ppermute x22, starting transfers between devices, fold(): lax.ppermute(value[r + 1], axis, p)  27.2 us
    all_gather x1, blocking collectives, body(): all_weight = lax.all_gather(weight, 'expert', axis=0, tiled=False)  18.1 us
    ppermute x16, starting transfers between devices, spread(): lax.ppermute(value, axis, [(b, a) for a, b in p])  14.9 us
    another operation x10, other arithmetic, spread(): jnp.stack([value] + [lax.ppermute(value, axis, [(b, a) for a, b in p]) fo...  13.8 us
    dot_general x2, matrix products, body(): gate_part = jnp.dot(gathered, w_gate[0], preferred_element_type=jnp.float32)  8.03 us
  transfers between devices with their start and end apart: 38, of which 16 were waited for; matrix products, arithmetic and copies ran while one was open for 33% of the time, Pallas kernels for 0%

profile of v2, /device:TPU:10, one launch (start us, length us, event | category | flops | bytes accessed | tf_op | source)
XLA Modules:
  0.0 214.6 jit_solution(10584739713312410121)
XLA Ops:
  0.0 0.7 fusion.42
  0.7 1.3 copy.52
  3.4 2.6 %collective-permute-start.1 = (bf16[16,4096]{1,0:T(8,128)(2,1)S(1)}, bf16[16,4096]{1,0:T(8,128)(2,1)S(1)}, u32[]{:S(2)}, u32[]{:S(2)}) collective-permute-start(bf16[16,4096]{1,0:T(8,128)(2,1)S(1)} %reshape.226), channel_id=1, source_target_pairs={{8,0},{9,1},{10,2},{11,3},{12,4},{13,5},{14,6},{15,7},{0,8},{1,9},... | collective-permute-start | bytes 393224 | tf_op jit(solution)/shard_map/ppermute | solution.py:21
  6.0 2.5 %collective-permute-start.2 = (bf16[16,4096]{1,0:T(8,128)(2,1)S(1)}, bf16[16,4096]{1,0:T(8,128)(2,1)S(1)}, u32[]{:S(2)}, u32[]{:S(2)}) collective-permute-start(bf16[16,4096]{1,0:T(8,128)(2,1)S(1)} %reshape.226), channel_id=1, source_target_pairs={{12,0},{13,1},{14,2},{15,3},{0,4},{1,5},{2,6},{3,7},{4,8},{5,9},{6... | collective-permute-start | bytes 393224 | tf_op jit(solution)/shard_map/ppermute | solution.py:21
  8.6 1.5 collective-permute-start.20
  11.8 2.4 %collective-permute-start.21 = (bf16[16,4096]{1,0:T(8,128)(2,1)S(1)}, bf16[16,4096]{1,0:T(8,128)(2,1)S(1)}, u32[]{:S(2)}, u32[]{:S(2)}) collective-permute-start(bf16[16,4096]{1,0:T(8,128)(2,1)S(1)} %reshape.230), channel_id=1, source_target_pairs={{12,0},{13,1},{14,2},{15,3},{0,4},{1,5},{2,6},{3,7},{4,8},{5,9},{6... | collective-permute-start | bytes 393224 | tf_op jit(solution)/shard_map/ppermute | solution.py:21
  14.2 1.5 collective-permute-done.1
  15.7 7.7 %collective-permute-done.2 = bf16[16,4096]{1,0:T(8,128)(2,1)S(1)} collective-permute-done((bf16[16,4096]{1,0:T(8,128)(2,1)S(1)}, bf16[16,4096]{1,0:T(8,128)(2,1)S(1)}, u32[]{:S(2)}, u32[]{:S(2)}) %collective-permute-start.2) | collective-permute-done | bytes 131104 | tf_op jit(solution)/shard_map/ppermute | solution.py:21
  23.6 1.6 collective-permute-start.5
  25.5 0.6 collective-permute-start.3
  26.5 3.6 %collective-permute-done.5 = bf16[4,16,2048]{2,1,0:T(8,128)(2,1)S(1)} collective-permute-done((bf16[4,16,2048]{2,1,0:T(8,128)(2,1)S(1)}, bf16[4,16,2048]{2,1,0:T(8,128)(2,1)S(1)}, u32[]{:S(2)}, u32[]{:S(2)}) %collective-permute-start.5) | collective-permute-done | bytes 262176 | tf_op jit(solution)/shard_map/ppermute | solution.py:21
  30.1 0.6 collective-permute-start.6
  30.7 3.7 %collective-permute-done.3 = bf16[4,16,2048]{2,1,0:T(8,128)(2,1)S(1)} collective-permute-done((bf16[4,16,2048]{2,1,0:T(8,128)(2,1)S(1)}, bf16[4,16,2048]{2,1,0:T(8,128)(2,1)S(1)}, u32[]{:S(2)}, u32[]{:S(2)}) %collective-permute-start.3) | collective-permute-done | bytes 262176 | tf_op jit(solution)/shard_map/ppermute | solution.py:21
  34.7 8.4 %collective-permute-done.6 = bf16[2,4,16,2048]{3,2,1,0:T(8,128)(2,1)S(1)} collective-permute-done((bf16[2,4,16,2048]{3,2,1,0:T(8,128)(2,1)S(1)}, bf16[2,4,16,2048]{3,2,1,0:T(8,128)(2,1)S(1)}, u32[]{:S(2)}, u32[]{:S(2)}) %collective-permute-start.6) | collective-permute-done | bytes 524320 | tf_op jit(solution)/shard_map/ppermute | solution.py:21
  43.2 0.5 collective-permute-done.4
  43.7 1.9 fusion.59
  45.6 0.8 slice_bitcast_fusion.35
  46.4 18.1 %all-gather = f32[256,4,16]{2,1,0:T(4,128)S(1)} all-gather(f32[16,4,16]{2,1,0:T(4,128)S(1)} %select_reduce_fusion.2), channel_id=2, replica_groups=mesh['dp'=2,'expert'=16] {'expert'}, dimensions={0}, use_global_device_ids=true | all-gather | bytes 69632 | tf_op jit(solution)/shard_map/all_gather | solution.py:46
  64.5 1.0 collective-permute-start.22
  66.0 0.7 copy-done.3
  66.7 1.8 fusion.54
  68.5 1.0 collective-permute-start.25
  69.5 4.4 %collective-permute-done.22 = bf16[4,16,2048]{2,1,0:T(8,128)(2,1)} collective-permute-done((bf16[4,16,2048]{2,1,0:T(8,128)(2,1)}, bf16[4,16,2048]{2,1,0:T(8,128)(2,1)}, u32[]{:S(2)}, u32[]{:S(2)}) %collective-permute-start.22) | collective-permute-done | bytes 262176 | tf_op jit(solution)/shard_map/ppermute | solution.py:21
  74.0 1.8 fusion.55
  75.8 0.5 collective-permute-start.23
  77.2 7.4 %collective-permute-done.25 = bf16[2,4,16,2048]{3,2,1,0:T(8,128)(2,1)} collective-permute-done((bf16[2,4,16,2048]{3,2,1,0:T(8,128)(2,1)}, bf16[2,4,16,2048]{3,2,1,0:T(8,128)(2,1)}, u32[]{:S(2)}, u32[]{:S(2)}) %collective-permute-start.25) | collective-permute-done | bytes 524320 | tf_op jit(solution)/shard_map/ppermute | solution.py:21
  84.6 1.1 maximum_bitcast_fusion.1
  85.8 3.1 %collective-permute-done.23 = bf16[2,4,16,2048]{3,2,1,0:T(8,128)(2,1)} collective-permute-done((bf16[2,4,16,2048]{3,2,1,0:T(8,128)(2,1)}, bf16[2,4,16,2048]{3,2,1,0:T(8,128)(2,1)}, u32[]{:S(2)}, u32[]{:S(2)}) %collective-permute-start.23) | collective-permute-done | bytes 524320 | tf_op jit(solution)/shard_map/ppermute | solution.py:21
  88.9 3.6 %fusion.58 = (bf16[1,2,2,4,16,4096]{5,4,3,1,2,0:T(8,128)(2,1)}, bf16[2,2,4,16,4096]{4,3,2,0,1:T(8,128)(2,1)}) fusion(bf16[2,2,4,16,2048]{4,3,2,0,1:T(8,128)(2,1)S(1)} %maximum_bitcast_fusion.1, bf16[1,2,4,16,2048]{4,3,2,0,1:T(8,128)(2,1)} %bitcast.50, bf16[1,2,4,16,2048]{4,3,2,0,1:T(8,128)(2,1)S(1)} %get-tuple-element.21), kind=kLoop, calls=%fused_computation.156 | loop fusion | flops 6291456 | bytes 6291456 | tf_op jit(solution)/shard_map/stack | solution.py:21
  92.5 2.1 pad_maximum_fusion
  95.2 2.0 copy-done.1
  97.2 3.5 %fusion.8 = f32[512,768]{1,0:T(8,128)S(1)} fusion(bf16[512,4096]{1,0:T(8,128)(2,1)S(1)} %bitcast.199, bf16[1,4096,768]{2,1,0:T(8,128)(2,1)S(1)} %bitcast.222), kind=kOutput, calls=%fused_computation.11 | convolution fusion | flops 3221225472 | bytes 12058624 | tf_op jit(solution)/shard_map/dot_general | solution.py:87
  100.6 16.7 %multiply_convert_fusion.1 = bf16[512,4096]{1,0:T(8,128)(2,1)} fusion(bf16[1,768,4096]{2,1,0:T(8,128)(2,1)} %param.17, f32[512]{0:T(512)S(1)} %mul.64, f32[512,768]{1,0:T(8,128)S(1)} %fusion.8, bf16[512,4096]{1,0:T(8,128)(2,1)} %bitcast.200, bf16[1,4096,768]{2,1,0:T(8,128)(2,1)} %param.16), kind=kOutput, calls=%fused_computation.2 | convolution fusion | flops 6449004544 | bytes 22546432 | tf_op jit(solution)/shard_map/dot_general | solution.py:90
  117.3 4.1 %fusion.60 = (bf16[256,4096]{1,0:T(8,128)(2,1)}, bf16[256,4096]{1,0:T(8,128)(2,1)S(1)}) fusion(bf16[512,4096]{1,0:T(8,128)(2,1)} %multiply_convert_fusion.1), kind=kLoop, calls=%fused_computation.158 | loop fusion | bytes 8388608 | tf_op jit(solution)/shard_map/slice | solution.py:25
  121.9 2.3 %pad_maximum_fusion.1 = bf16[2,2,2,4,16,4096]{5,4,3,1,2,0:T(8,128)(2,1)S(1)} fusion(bf16[1,2,2,4,16,4096]{5,4,3,1,2,0:T(8,128)(2,1)} %bitcast.57, bf16[1,2,2,4,16,4096]{5,4,3,1,2,0:T(8,128)(2,1)S(1)} %copy-done), kind=kLoop, calls=%fused_computation.14 | loop fusion | flops 2097152 | bytes 8388608 | tf_op jit(solution)/shard_map/stack | solution.py:21
  124.8 2.0 copy-done.2
  126.8 4.6 %fusion.6 = f32[512,768]{1,0:T(8,128)} fusion(bf16[512,4096]{1,0:T(8,128)(2,1)S(1)} %bitcast.201, bf16[1,4096,768]{2,1,0:T(8,128)(2,1)S(1)} %bitcast.224), kind=kOutput, calls=%fused_computation.9 | convolution fusion | flops 3221225472 | bytes 12058624 | tf_op jit(solution)/shard_map/dot_general | solution.py:87
  131.4 17.1 %multiply_convert_fusion = bf16[512,4096]{1,0:T(8,128)(2,1)} fusion(bf16[1,768,4096]{2,1,0:T(8,128)(2,1)} %param.17, f32[512]{0:T(512)S(1)} %mul.69, f32[512,768]{1,0:T(8,128)} %fusion.6, bf16[512,4096]{1,0:T(8,128)(2,1)} %bitcast.202, bf16[1,4096,768]{2,1,0:T(8,128)(2,1)} %param.16), kind=kOutput, calls=%fused_computation.1 | convolution fusion | flops 6449004544 | bytes 22546432 | tf_op jit(solution)/shard_map/dot_general | solution.py:90
  148.5 2.7 %fusion.61 = (bf16[256,4096]{1,0:T(8,128)(2,1)S(1)}, bf16[256,4096]{1,0:T(8,128)(2,1)S(1)}) fusion(bf16[512,4096]{1,0:T(8,128)(2,1)} %multiply_convert_fusion), kind=kLoop, calls=%fused_computation.159 | loop fusion | bytes 8388608 | tf_op jit(solution)/shard_map/slice | solution.py:25
  151.3 2.4 %fusion.11 = bf16[2,2,4,16,4096]{4,3,2,1,0:T(8,128)(2,1)S(1)} fusion(bf16[2,2,4,16,4096]{4,3,2,1,0:T(8,128)(2,1)S(1)} %bitcast.197, bf16[2,2,4,16,4096]{4,3,2,1,0:T(8,128)(2,1)} %collective-permute-done.8), kind=kLoop, calls=%fused_computation.18 | loop fusion | flops 4194304 | bytes 6291456 | tf_op jit(solution)/shard_map/convert_element_type | solution.py:10
  153.8 1.1 collective-permute-start.9
  154.9 1.5 collective-permute-start.14
  156.5 0.8 fusion.10
  157.4 0.6 collective-permute-start.28
  158.1 1.1 collective-permute-start.33
  159.2 9.4 %collective-permute-done.9 = bf16[2,4,16,2048]{3,2,1,0:T(8,128)(2,1)S(1)} collective-permute-done((bf16[2,4,16,2048]{3,2,1,0:T(8,128)(2,1)S(1)}, bf16[2,4,16,2048]{3,2,1,0:T(8,128)(2,1)S(1)}, u32[]{:S(2)}, u32[]{:S(2)}) %collective-permute-start.9) | collective-permute-done | bytes 524320 | tf_op jit(solution)/shard_map/ppermute | solution.py:25
  168.7 1.1 collective-permute-start.10
  170.0 1.6 collective-permute-start.15
  171.5 8.3 %collective-permute-done.28 = bf16[2,4,16,2048]{3,2,1,0:T(8,128)(2,1)S(1)} collective-permute-done((bf16[2,4,16,2048]{3,2,1,0:T(8,128)(2,1)S(1)}, bf16[2,4,16,2048]{3,2,1,0:T(8,128)(2,1)S(1)}, u32[]{:S(2)}, u32[]{:S(2)}) %collective-permute-start.28) | collective-permute-done | bytes 524320 | tf_op jit(solution)/shard_map/ppermute | solution.py:25
  180.0 1.1 collective-permute-start.29
  181.2 1.6 collective-permute-start.34
  182.8 3.8 %collective-permute-done.10 = bf16[4,16,2048]{2,1,0:T(8,128)(2,1)S(1)} collective-permute-done((bf16[4,16,2048]{2,1,0:T(8,128)(2,1)S(1)}, bf16[4,16,2048]{2,1,0:T(8,128)(2,1)S(1)}, u32[]{:S(2)}, u32[]{:S(2)}) %collective-permute-start.10) | collective-permute-done | bytes 262176 | tf_op jit(solution)/shard_map/ppermute | solution.py:25
  186.7 1.0 collective-permute-start.11
  187.7 4.7 %collective-permute-start.12 = (bf16[16,2048]{1,0:T(8,128)(2,1)S(1)}, bf16[16,2048]{1,0:T(8,128)(2,1)S(1)}, u32[]{:S(2)}, u32[]{:S(2)}) collective-permute-start(bf16[16,2048]{1,0:T(8,128)(2,1)S(1)} %get-tuple-element.31), channel_id=1, source_target_pairs={{0,8},{1,9},{2,10},{3,11},{4,12},{5,13},{6,14},{7,15},{8,0},{9,1},... | collective-permute-start | bytes 196616 | tf_op jit(solution)/shard_map/ppermute | solution.py:25
  192.5 2.1 collective-permute-start.16
  194.7 2.6 %collective-permute-start.17 = (bf16[16,2048]{1,0:T(8,128)(2,1)S(1)}, bf16[16,2048]{1,0:T(8,128)(2,1)S(1)}, u32[]{:S(2)}, u32[]{:S(2)}) collective-permute-start(bf16[16,2048]{1,0:T(8,128)(2,1)S(1)} %get-tuple-element.34), channel_id=1, source_target_pairs={{0,8},{1,9},{2,10},{3,11},{4,12},{5,13},{6,14},{7,15},{8,0},{9,1},... | collective-permute-start | bytes 196616 | tf_op jit(solution)/shard_map/ppermute | solution.py:25
  197.5 2.0 collective-permute-start.30
  199.5 2.2 %collective-permute-start.31 = (bf16[16,2048]{1,0:T(8,128)(2,1)S(1)}, bf16[16,2048]{1,0:T(8,128)(2,1)S(1)}, u32[]{:S(2)}, u32[]{:S(2)}) collective-permute-start(bf16[16,2048]{1,0:T(8,128)(2,1)S(1)} %get-tuple-element.39), channel_id=1, source_target_pairs={{0,8},{1,9},{2,10},{3,11},{4,12},{5,13},{6,14},{7,15},{8,0},{9,1},... | collective-permute-start | bytes 196616 | tf_op jit(solution)/shard_map/ppermute | solution.py:25
  201.8 2.0 collective-permute-start.35
  203.8 2.6 %collective-permute-done.18 = bf16[16,2048]{1,0:T(8,128)(2,1)S(1)} collective-permute-done((bf16[16,2048]{1,0:T(8,128)(2,1)S(1)}, bf16[16,2048]{1,0:T(8,128)(2,1)S(1)}, u32[]{:S(2)}, u32[]{:S(2)}) %collective-permute-start.18) | collective-permute-done | bytes 65568 | tf_op jit(solution)/shard_map/ppermute | solution.py:25
  206.8 3.7 %collective-permute-done.32 = bf16[16,2048]{1,0:T(8,128)(2,1)S(1)} collective-permute-done((bf16[16,2048]{1,0:T(8,128)(2,1)S(1)}, bf16[16,2048]{1,0:T(8,128)(2,1)S(1)}, u32[]{:S(2)}, u32[]{:S(2)}) %collective-permute-start.32) | collective-permute-done | bytes 65568 | tf_op jit(solution)/shard_map/ppermute | solution.py:25
  210.8 0.9 collective-permute-done.36
  211.6 1.9 collective-permute-done.37
  213.7 1.0 pad_maximum_fusion.10
  (134 shorter events, 8.8 us)
Async XLA Ops:
  0.0 10.8 %copy-start.4 = (f32[16,4,8]{0,2,1:T(8,128)S(1)}, f32[16,4,8]{0,2,1:T(8,128)}, u32[]{:S(2)}) copy-start(f32[16,4,8]{0,2,1:T(8,128)} %param.11) | copy-start | bytes 6148
  0.0 11.0 %copy-start.5 = (s32[16,4,8]{0,2,1:T(8,128)S(1)}, s32[16,4,8]{0,2,1:T(8,128)}, u32[]{:S(2)}) copy-start(s32[16,4,8]{0,2,1:T(8,128)} %param.10) | copy-start | bytes 6148
  0.0 11.7 %copy-start.6 = (s32[16]{0:T(128)S(1)}, s32[16]{0:T(128)}, u32[]{:S(2)}) copy-start(s32[16]{0:T(128)} %param.12) | copy-start | bytes 196
  2.9 8.9 %collective-permute-start = (bf16[16,4096]{1,0:T(8,128)(2,1)S(1)}, bf16[16,4096]{1,0:T(8,128)(2,1)S(1)}, u32[]{:S(2)}, u32[]{:S(2)}) collective-permute-start(bf16[16,4096]{1,0:T(8,128)(2,1)S(1)} %reshape.226), channel_id=1, source_target_pairs={{4,0},{5,1},{6,2},{7,3},{8,4},{9,5},{10,6},{11,7},{12,8},{13,9},{1... | collective-permute-start | bytes 393224 | tf_op jit(solution)/shard_map/ppermute | solution.py:21
  3.4 12.3 %collective-permute-start.1 = (bf16[16,4096]{1,0:T(8,128)(2,1)S(1)}, bf16[16,4096]{1,0:T(8,128)(2,1)S(1)}, u32[]{:S(2)}, u32[]{:S(2)}) collective-permute-start(bf16[16,4096]{1,0:T(8,128)(2,1)S(1)} %reshape.226), channel_id=1, source_target_pairs={{8,0},{9,1},{10,2},{11,3},{12,4},{13,5},{14,6},{15,7},{0,8},{1,9},... | collective-permute-start | bytes 393224 | tf_op jit(solution)/shard_map/ppermute | solution.py:21
  6.0 17.4 %collective-permute-start.2 = (bf16[16,4096]{1,0:T(8,128)(2,1)S(1)}, bf16[16,4096]{1,0:T(8,128)(2,1)S(1)}, u32[]{:S(2)}, u32[]{:S(2)}) collective-permute-start(bf16[16,4096]{1,0:T(8,128)(2,1)S(1)} %reshape.226), channel_id=1, source_target_pairs={{12,0},{13,1},{14,2},{15,3},{0,4},{1,5},{2,6},{3,7},{4,8},{5,9},{6... | collective-permute-start | bytes 393224 | tf_op jit(solution)/shard_map/ppermute | solution.py:21
  8.5 26.1 %collective-permute-start.19 = (bf16[16,4096]{1,0:T(8,128)(2,1)S(1)}, bf16[16,4096]{1,0:T(8,128)(2,1)S(1)}, u32[]{:S(2)}, u32[]{:S(2)}) collective-permute-start(bf16[16,4096]{1,0:T(8,128)(2,1)S(1)} %reshape.230), channel_id=1, source_target_pairs={{4,0},{5,1},{6,2},{7,3},{8,4},{9,5},{10,6},{11,7},{12,8},{13,9},{1... | collective-permute-start | bytes 393224 | tf_op jit(solution)/shard_map/ppermute | solution.py:21
  8.6 26.0 %collective-permute-start.20 = (bf16[16,4096]{1,0:T(8,128)(2,1)S(1)}, bf16[16,4096]{1,0:T(8,128)(2,1)S(1)}, u32[]{:S(2)}, u32[]{:S(2)}) collective-permute-start(bf16[16,4096]{1,0:T(8,128)(2,1)S(1)} %reshape.230), channel_id=1, source_target_pairs={{8,0},{9,1},{10,2},{11,3},{12,4},{13,5},{14,6},{15,7},{0,8},{1,9},... | collective-permute-start | bytes 393224 | tf_op jit(solution)/shard_map/ppermute | solution.py:21
  11.8 22.8 %collective-permute-start.21 = (bf16[16,4096]{1,0:T(8,128)(2,1)S(1)}, bf16[16,4096]{1,0:T(8,128)(2,1)S(1)}, u32[]{:S(2)}, u32[]{:S(2)}) collective-permute-start(bf16[16,4096]{1,0:T(8,128)(2,1)S(1)} %reshape.230), channel_id=1, source_target_pairs={{12,0},{13,1},{14,2},{15,3},{0,4},{1,5},{2,6},{3,7},{4,8},{5,9},{6... | collective-permute-start | bytes 393224 | tf_op jit(solution)/shard_map/ppermute | solution.py:21
  23.6 6.4 %collective-permute-start.5 = (bf16[4,16,2048]{2,1,0:T(8,128)(2,1)S(1)}, bf16[4,16,2048]{2,1,0:T(8,128)(2,1)S(1)}, u32[]{:S(2)}, u32[]{:S(2)}) collective-permute-start(bf16[4,16,2048]{2,1,0:T(8,128)(2,1)S(1)} %get-tuple-element.17), channel_id=1, source_target_pairs={{16,0},{0,16},{17,1},{1,17},{18,2},{2,18},{19,3},{3,19},{20,4},{4,... | collective-permute-start | bytes 786440 | tf_op jit(solution)/shard_map/ppermute | solution.py:21
  25.5 9.0 %collective-permute-start.3 = (bf16[4,16,2048]{2,1,0:T(8,128)(2,1)S(1)}, bf16[4,16,2048]{2,1,0:T(8,128)(2,1)S(1)}, u32[]{:S(2)}, u32[]{:S(2)}) collective-permute-start(bf16[4,16,2048]{2,1,0:T(8,128)(2,1)S(1)} %get-tuple-element.18), channel_id=1, source_target_pairs={{2,0},{3,1},{0,2},{1,3},{6,4},{7,5},{4,6},{5,7},{10,8},{11,9},{8,1... | collective-permute-start | bytes 786440 | tf_op jit(solution)/shard_map/ppermute | solution.py:21
  30.1 13.0 %collective-permute-start.6 = (bf16[2,4,16,2048]{3,2,1,0:T(8,128)(2,1)S(1)}, bf16[2,4,16,2048]{3,2,1,0:T(8,128)(2,1)S(1)}, u32[]{:S(2)}, u32[]{:S(2)}) collective-permute-start(bf16[2,4,16,2048]{3,2,1,0:T(8,128)(2,1)S(1)} %get-tuple-element.20), channel_id=1, source_target_pairs={{2,0},{3,1},{0,2},{1,3},{6,4},{7,5},{4,6},{5,7},{10,8},{11,9},{8,1... | collective-permute-start | bytes 1572872 | tf_op jit(solution)/shard_map/ppermute | solution.py:21
  34.5 9.2 %collective-permute-start.4 = (bf16[2,4,16,2048]{3,2,1,0:T(8,128)(2,1)S(1)}, bf16[2,4,16,2048]{3,2,1,0:T(8,128)(2,1)S(1)}, u32[]{:S(2)}, u32[]{:S(2)}) collective-permute-start(bf16[2,4,16,2048]{3,2,1,0:T(8,128)(2,1)S(1)} %get-tuple-element.14), channel_id=1, source_target_pairs={{16,0},{0,16},{17,1},{1,17},{18,2},{2,18},{19,3},{3,19},{20,4},{4,... | collective-permute-start | bytes 1572872 | tf_op jit(solution)/shard_map/ppermute | solution.py:21
  45.6 46.9 %collective-permute-start.7 = (bf16[2,2,4,16,4096]{4,3,2,0,1:T(8,128)(2,1)}, bf16[2,2,4,16,4096]{4,3,2,0,1:T(8,128)(2,1)}, u32[]{:S(2)}, u32[]{:S(2)}) collective-permute-start(bf16[2,2,4,16,4096]{4,3,2,0,1:T(8,128)(2,1)} %get-tuple-element.10), channel_id=1, source_target_pairs={{1,0},{0,1},{3,2},{2,3},{5,4},{4,5},{7,6},{6,7},{9,8},{8,9},{11,10... | collective-permute-start | bytes 6291464 | tf_op jit(solution)/shard_map/ppermute | solution.py:21
  46.4 19.6 %collective-permute-start.24 = (bf16[4,16,2048]{2,1,0:T(8,128)(2,1)S(1)}, bf16[4,16,2048]{2,1,0:T(8,128)(2,1)S(1)}, u32[]{:S(2)}, u32[]{:S(2)}) collective-permute-start(bf16[4,16,2048]{2,1,0:T(8,128)(2,1)S(1)} %get-tuple-element.25), channel_id=1, source_target_pairs={{16,0},{0,16},{17,1},{1,17},{18,2},{2,18},{19,3},{3,19},{20,4},{4,... | collective-permute-start | bytes 786440 | tf_op jit(solution)/shard_map/ppermute | solution.py:21
  64.5 9.4 %collective-permute-start.22 = (bf16[4,16,2048]{2,1,0:T(8,128)(2,1)}, bf16[4,16,2048]{2,1,0:T(8,128)(2,1)}, u32[]{:S(2)}, u32[]{:S(2)}) collective-permute-start(bf16[4,16,2048]{2,1,0:T(8,128)(2,1)} %get-tuple-element.26), channel_id=1, source_target_pairs={{2,0},{3,1},{0,2},{1,3},{6,4},{7,5},{4,6},{5,7},{10,8},{11,9},{8,1... | collective-permute-start | bytes 786440 | tf_op jit(solution)/shard_map/ppermute | solution.py:21
  66.0 0.7 copy-start.3
  68.5 16.1 %collective-permute-start.25 = (bf16[2,4,16,2048]{3,2,1,0:T(8,128)(2,1)}, bf16[2,4,16,2048]{3,2,1,0:T(8,128)(2,1)}, u32[]{:S(2)}, u32[]{:S(2)}) collective-permute-start(bf16[2,4,16,2048]{3,2,1,0:T(8,128)(2,1)} %get-tuple-element.28), channel_id=1, source_target_pairs={{2,0},{3,1},{0,2},{1,3},{6,4},{7,5},{4,6},{5,7},{10,8},{11,9},{8,1... | collective-permute-start | bytes 1572872 | tf_op jit(solution)/shard_map/ppermute | solution.py:21
  75.8 13.1 %collective-permute-start.23 = (bf16[2,4,16,2048]{3,2,1,0:T(8,128)(2,1)}, bf16[2,4,16,2048]{3,2,1,0:T(8,128)(2,1)}, u32[]{:S(2)}, u32[]{:S(2)}) collective-permute-start(bf16[2,4,16,2048]{3,2,1,0:T(8,128)(2,1)} %get-tuple-element.22), channel_id=1, source_target_pairs={{16,0},{0,16},{17,1},{1,17},{18,2},{2,18},{19,3},{3,19},{20,4},{4,... | collective-permute-start | bytes 1572872 | tf_op jit(solution)/shard_map/ppermute | solution.py:21
  92.5 29.4 %collective-permute-start.26 = (bf16[2,2,4,16,4096]{4,3,2,0,1:T(8,128)(2,1)}, bf16[2,2,4,16,4096]{4,3,2,0,1:T(8,128)(2,1)}, u32[]{:S(2)}, u32[]{:S(2)}) collective-permute-start(bf16[2,2,4,16,4096]{4,3,2,0,1:T(8,128)(2,1)} %get-tuple-element.12), channel_id=1, source_target_pairs={{1,0},{0,1},{3,2},{2,3},{5,4},{4,5},{7,6},{6,7},{9,8},{8,9},{11,10... | collective-permute-start | bytes 6291464 | tf_op jit(solution)/shard_map/ppermute | solution.py:21
  92.5 4.6 %slice-start = ((s8[6291456]{0:T(1024)(128)(4,1)}), s8[4194304]{0:T(1024)(128)(4,1)S(1)}, s32[]{:S(2)}) async-start(s8[6291456]{0:T(1024)(128)(4,1)} %bitcast.221), calls=%async_computation | async-start | bytes 8388608
  94.7 2.5 %slice-start.1 = ((s8[6291456]{0:T(1024)(128)(4,1)}), s8[2097152]{0:T(1024)(128)(4,1)S(1)}, s32[]{:S(2)}) async-start(s8[6291456]{0:T(1024)(128)(4,1)} %bitcast.221), calls=%async_computation.1 | async-start | bytes 4194304
  95.2 2.0 copy-start.1
  117.3 4.6 %copy-start = (bf16[1,2,2,4,16,4096]{5,4,3,1,2,0:T(8,128)(2,1)S(1)}, bf16[1,2,2,4,16,4096]{5,4,3,1,2,0:T(8,128)(2,1)}, u32[]{:S(2)}) copy-start(bf16[1,2,2,4,16,4096]{5,4,3,1,2,0:T(8,128)(2,1)} %get-tuple-element.11) | copy-start | bytes 6291460
  121.4 29.9 %collective-permute-start.8 = (bf16[2,2,4,16,4096]{4,3,2,1,0:T(8,128)(2,1)}, bf16[2,2,4,16,4096]{4,3,2,1,0:T(8,128)(2,1)}, u32[]{:S(2)}, u32[]{:S(2)}) collective-permute-start(bf16[2,2,4,16,4096]{4,3,2,1,0:T(8,128)(2,1)} %bitcast.25), channel_id=1, source_target_pairs={{0,1},{1,0},{2,3},{3,2},{4,5},{5,4},{6,7},{7,6},{8,9},{9,8},{10,11... | collective-permute-start | bytes 6291464 | tf_op jit(solution)/shard_map/ppermute | solution.py:25
  121.9 4.9 %slice-start.2 = ((s8[6291456]{0:T(1024)(128)(4,1)}), s8[4194304]{0:T(1024)(128)(4,1)S(1)}, s32[]{:S(2)}) async-start(s8[6291456]{0:T(1024)(128)(4,1)} %bitcast.223), calls=%async_computation.2 | async-start | bytes 8388608
  124.3 2.5 %slice-start.3 = ((s8[6291456]{0:T(1024)(128)(4,1)}), s8[2097152]{0:T(1024)(128)(4,1)S(1)}, s32[]{:S(2)}) async-start(s8[6291456]{0:T(1024)(128)(4,1)} %bitcast.223), calls=%async_computation.3 | async-start | bytes 4194304
  124.8 2.0 copy-start.2
  151.2 5.3 %collective-permute-start.27 = (bf16[2,2,4,16,4096]{4,3,2,1,0:T(8,128)(2,1)S(1)}, bf16[2,2,4,16,4096]{4,3,2,1,0:T(8,128)(2,1)S(1)}, u32[]{:S(2)}, u32[]{:S(2)}) collective-permute-start(bf16[2,2,4,16,4096]{4,3,2,1,0:T(8,128)(2,1)S(1)} %bitcast.205), channel_id=1, source_target_pairs={{0,1},{1,0},{2,3},{3,2},{4,5},{5,4},{6,7},{7,6},{8,9},{9,8},{10,11... | collective-permute-start | bytes 6291464 | tf_op jit(solution)/shard_map/ppermute | solution.py:25
  153.8 14.8 %collective-permute-start.9 = (bf16[2,4,16,2048]{3,2,1,0:T(8,128)(2,1)S(1)}, bf16[2,4,16,2048]{3,2,1,0:T(8,128)(2,1)S(1)}, u32[]{:S(2)}, u32[]{:S(2)}) collective-permute-start(bf16[2,4,16,2048]{3,2,1,0:T(8,128)(2,1)S(1)} %slice_bitcast_fusion.8), channel_id=1, source_target_pairs={{0,2},{1,3},{2,0},{3,1},{4,6},{5,7},{6,4},{7,5},{8,10},{9,11},{10,... | collective-permute-start | bytes 1572872 | tf_op jit(solution)/shard_map/ppermute | solution.py:25
  154.9 14.9 %collective-permute-start.14 = (bf16[2,4,16,2048]{3,2,1,0:T(8,128)(2,1)S(1)}, bf16[2,4,16,2048]{3,2,1,0:T(8,128)(2,1)S(1)}, u32[]{:S(2)}, u32[]{:S(2)}) collective-permute-start(bf16[2,4,16,2048]{3,2,1,0:T(8,128)(2,1)S(1)} %slice_bitcast_fusion.6), channel_id=1, source_target_pairs={{0,16},{16,0},{1,17},{17,1},{2,18},{18,2},{3,19},{19,3},{4,20},{20... | collective-permute-start | bytes 1572872 | tf_op jit(solution)/shard_map/ppermute | solution.py:25
  157.4 22.4 %collective-permute-start.28 = (bf16[2,4,16,2048]{3,2,1,0:T(8,128)(2,1)S(1)}, bf16[2,4,16,2048]{3,2,1,0:T(8,128)(2,1)S(1)}, u32[]{:S(2)}, u32[]{:S(2)}) collective-permute-start(bf16[2,4,16,2048]{3,2,1,0:T(8,128)(2,1)S(1)} %slice_bitcast_fusion.4), channel_id=1, source_target_pairs={{0,2},{1,3},{2,0},{3,1},{4,6},{5,7},{6,4},{7,5},{8,10},{9,11},{10,... | collective-permute-start | bytes 1572872 | tf_op jit(solution)/shard_map/ppermute | solution.py:25
  158.1 23.0 %collective-permute-start.33 = (bf16[2,4,16,2048]{3,2,1,0:T(8,128)(2,1)S(1)}, bf16[2,4,16,2048]{3,2,1,0:T(8,128)(2,1)S(1)}, u32[]{:S(2)}, u32[]{:S(2)}) collective-permute-start(bf16[2,4,16,2048]{3,2,1,0:T(8,128)(2,1)S(1)} %slice_bitcast_fusion.2), channel_id=1, source_target_pairs={{0,16},{16,0},{1,17},{17,1},{2,18},{18,2},{3,19},{19,3},{4,20},{20... | collective-permute-start | bytes 1572872 | tf_op jit(solution)/shard_map/ppermute | solution.py:25
  168.7 17.9 %collective-permute-start.10 = (bf16[4,16,2048]{2,1,0:T(8,128)(2,1)S(1)}, bf16[4,16,2048]{2,1,0:T(8,128)(2,1)S(1)}, u32[]{:S(2)}, u32[]{:S(2)}) collective-permute-start(bf16[4,16,2048]{2,1,0:T(8,128)(2,1)S(1)} %slice_bitcast_fusion.16), channel_id=1, source_target_pairs={{0,16},{16,0},{1,17},{17,1},{2,18},{18,2},{3,19},{19,3},{4,20},{20... | collective-permute-start | bytes 786440 | tf_op jit(solution)/shard_map/ppermute | solution.py:25
  170.0 22.4 %collective-permute-start.15 = (bf16[4,16,2048]{2,1,0:T(8,128)(2,1)S(1)}, bf16[4,16,2048]{2,1,0:T(8,128)(2,1)S(1)}, u32[]{:S(2)}, u32[]{:S(2)}) collective-permute-start(bf16[4,16,2048]{2,1,0:T(8,128)(2,1)S(1)} %slice_bitcast_fusion.14), channel_id=1, source_target_pairs={{0,2},{1,3},{2,0},{3,1},{4,6},{5,7},{6,4},{7,5},{8,10},{9,11},{10,... | collective-permute-start | bytes 786440 | tf_op jit(solution)/shard_map/ppermute | solution.py:25
  180.0 12.5 %collective-permute-start.29 = (bf16[4,16,2048]{2,1,0:T(8,128)(2,1)S(1)}, bf16[4,16,2048]{2,1,0:T(8,128)(2,1)S(1)}, u32[]{:S(2)}, u32[]{:S(2)}) collective-permute-start(bf16[4,16,2048]{2,1,0:T(8,128)(2,1)S(1)} %slice_bitcast_fusion.12), channel_id=1, source_target_pairs={{0,16},{16,0},{1,17},{17,1},{2,18},{18,2},{3,19},{19,3},{4,20},{20... | collective-permute-start | bytes 786440 | tf_op jit(solution)/shard_map/ppermute | solution.py:25
  181.2 13.4 %collective-permute-start.34 = (bf16[4,16,2048]{2,1,0:T(8,128)(2,1)S(1)}, bf16[4,16,2048]{2,1,0:T(8,128)(2,1)S(1)}, u32[]{:S(2)}, u32[]{:S(2)}) collective-permute-start(bf16[4,16,2048]{2,1,0:T(8,128)(2,1)S(1)} %slice_bitcast_fusion.10), channel_id=1, source_target_pairs={{0,2},{1,3},{2,0},{3,1},{4,6},{5,7},{6,4},{7,5},{8,10},{9,11},{10,... | collective-permute-start | bytes 786440 | tf_op jit(solution)/shard_map/ppermute | solution.py:25
  186.7 10.7 %collective-permute-start.11 = (bf16[16,2048]{1,0:T(8,128)(2,1)S(1)}, bf16[16,2048]{1,0:T(8,128)(2,1)S(1)}, u32[]{:S(2)}, u32[]{:S(2)}) collective-permute-start(bf16[16,2048]{1,0:T(8,128)(2,1)S(1)} %get-tuple-element.29), channel_id=1, source_target_pairs={{0,4},{1,5},{2,6},{3,7},{4,8},{5,9},{6,10},{7,11},{8,12},{9,13},{1... | collective-permute-start | bytes 196616 | tf_op jit(solution)/shard_map/ppermute | solution.py:25
  187.7 9.8 %collective-permute-start.12 = (bf16[16,2048]{1,0:T(8,128)(2,1)S(1)}, bf16[16,2048]{1,0:T(8,128)(2,1)S(1)}, u32[]{:S(2)}, u32[]{:S(2)}) collective-permute-start(bf16[16,2048]{1,0:T(8,128)(2,1)S(1)} %get-tuple-element.31), channel_id=1, source_target_pairs={{0,8},{1,9},{2,10},{3,11},{4,12},{5,13},{6,14},{7,15},{8,0},{9,1},... | collective-permute-start | bytes 196616 | tf_op jit(solution)/shard_map/ppermute | solution.py:25
  192.4 7.1 %collective-permute-start.13 = (bf16[16,2048]{1,0:T(8,128)(2,1)S(1)}, bf16[16,2048]{1,0:T(8,128)(2,1)S(1)}, u32[]{:S(2)}, u32[]{:S(2)}) collective-permute-start(bf16[16,2048]{1,0:T(8,128)(2,1)S(1)} %get-tuple-element.30), channel_id=1, source_target_pairs={{0,12},{1,13},{2,14},{3,15},{4,0},{5,1},{6,2},{7,3},{8,4},{9,5},{1... | collective-permute-start | bytes 196616 | tf_op jit(solution)/shard_map/ppermute | solution.py:25
  192.5 9.2 %collective-permute-start.16 = (bf16[16,2048]{1,0:T(8,128)(2,1)S(1)}, bf16[16,2048]{1,0:T(8,128)(2,1)S(1)}, u32[]{:S(2)}, u32[]{:S(2)}) collective-permute-start(bf16[16,2048]{1,0:T(8,128)(2,1)S(1)} %get-tuple-element.32), channel_id=1, source_target_pairs={{0,4},{1,5},{2,6},{3,7},{4,8},{5,9},{6,10},{7,11},{8,12},{9,13},{1... | collective-permute-start | bytes 196616 | tf_op jit(solution)/shard_map/ppermute | solution.py:25
  194.7 7.1 %collective-permute-start.17 = (bf16[16,2048]{1,0:T(8,128)(2,1)S(1)}, bf16[16,2048]{1,0:T(8,128)(2,1)S(1)}, u32[]{:S(2)}, u32[]{:S(2)}) collective-permute-start(bf16[16,2048]{1,0:T(8,128)(2,1)S(1)} %get-tuple-element.34), channel_id=1, source_target_pairs={{0,8},{1,9},{2,10},{3,11},{4,12},{5,13},{6,14},{7,15},{8,0},{9,1},... | collective-permute-start | bytes 196616 | tf_op jit(solution)/shard_map/ppermute | solution.py:25
  197.4 9.0 %collective-permute-start.18 = (bf16[16,2048]{1,0:T(8,128)(2,1)S(1)}, bf16[16,2048]{1,0:T(8,128)(2,1)S(1)}, u32[]{:S(2)}, u32[]{:S(2)}) collective-permute-start(bf16[16,2048]{1,0:T(8,128)(2,1)S(1)} %get-tuple-element.33), channel_id=1, source_target_pairs={{0,12},{1,13},{2,14},{3,15},{4,0},{5,1},{6,2},{7,3},{8,4},{9,5},{1... | collective-permute-start | bytes 196616 | tf_op jit(solution)/shard_map/ppermute | solution.py:25
  197.5 9.3 %collective-permute-start.30 = (bf16[16,2048]{1,0:T(8,128)(2,1)S(1)}, bf16[16,2048]{1,0:T(8,128)(2,1)S(1)}, u32[]{:S(2)}, u32[]{:S(2)}) collective-permute-start(bf16[16,2048]{1,0:T(8,128)(2,1)S(1)} %get-tuple-element.37), channel_id=1, source_target_pairs={{0,4},{1,5},{2,6},{3,7},{4,8},{5,9},{6,10},{7,11},{8,12},{9,13},{1... | collective-permute-start | bytes 196616 | tf_op jit(solution)/shard_map/ppermute | solution.py:25
  199.5 7.4 %collective-permute-start.31 = (bf16[16,2048]{1,0:T(8,128)(2,1)S(1)}, bf16[16,2048]{1,0:T(8,128)(2,1)S(1)}, u32[]{:S(2)}, u32[]{:S(2)}) collective-permute-start(bf16[16,2048]{1,0:T(8,128)(2,1)S(1)} %get-tuple-element.39), channel_id=1, source_target_pairs={{0,8},{1,9},{2,10},{3,11},{4,12},{5,13},{6,14},{7,15},{8,0},{9,1},... | collective-permute-start | bytes 196616 | tf_op jit(solution)/shard_map/ppermute | solution.py:25
  201.7 8.9 %collective-permute-start.32 = (bf16[16,2048]{1,0:T(8,128)(2,1)S(1)}, bf16[16,2048]{1,0:T(8,128)(2,1)S(1)}, u32[]{:S(2)}, u32[]{:S(2)}) collective-permute-start(bf16[16,2048]{1,0:T(8,128)(2,1)S(1)} %get-tuple-element.38), channel_id=1, source_target_pairs={{0,12},{1,13},{2,14},{3,15},{4,0},{5,1},{6,2},{7,3},{8,4},{9,5},{1... | collective-permute-start | bytes 196616 | tf_op jit(solution)/shard_map/ppermute | solution.py:25
  201.8 9.0 %collective-permute-start.35 = (bf16[16,2048]{1,0:T(8,128)(2,1)S(1)}, bf16[16,2048]{1,0:T(8,128)(2,1)S(1)}, u32[]{:S(2)}, u32[]{:S(2)}) collective-permute-start(bf16[16,2048]{1,0:T(8,128)(2,1)S(1)} %get-tuple-element.40), channel_id=1, source_target_pairs={{0,4},{1,5},{2,6},{3,7},{4,8},{5,9},{6,10},{7,11},{8,12},{9,13},{1... | collective-permute-start | bytes 196616 | tf_op jit(solution)/shard_map/ppermute | solution.py:25
  206.4 5.3 %collective-permute-start.36 = (bf16[16,2048]{1,0:T(8,128)(2,1)S(1)}, bf16[16,2048]{1,0:T(8,128)(2,1)S(1)}, u32[]{:S(2)}, u32[]{:S(2)}) collective-permute-start(bf16[16,2048]{1,0:T(8,128)(2,1)S(1)} %get-tuple-element.42), channel_id=1, source_target_pairs={{0,8},{1,9},{2,10},{3,11},{4,12},{5,13},{6,14},{7,15},{8,0},{9,1},... | collective-permute-start | bytes 196616 | tf_op jit(solution)/shard_map/ppermute | solution.py:25
  206.7 6.8 %collective-permute-start.37 = (bf16[16,2048]{1,0:T(8,128)(2,1)S(1)}, bf16[16,2048]{1,0:T(8,128)(2,1)S(1)}, u32[]{:S(2)}, u32[]{:S(2)}) collective-permute-start(bf16[16,2048]{1,0:T(8,128)(2,1)S(1)} %get-tuple-element.41), channel_id=1, source_target_pairs={{0,12},{1,13},{2,14},{3,15},{4,0},{5,1},{6,2},{7,3},{8,4},{9,5},{1... | collective-permute-start | bytes 196616 | tf_op jit(solution)/shard_map/ppermute | solution.py:25
